TPU v7x, 512 devices: a whole 4x8x8 slice. The times are simulated.
512 devices in a mesh: vocab: 32 (over x, z), tok: 16 (over y, core).
Axes of the slice: x: 4, y: 8, z: 8, core: 2. Of those that a mesh axis runs over, the one named last changes fastest.
Arguments:
- embeddings: bfloat16 [131072, 4096], P('tok', 'vocab'), may hold values from -40 to 40
- norm_gain: bfloat16 [4096], P('vocab'), may hold values from 0.5 to 1.5
- query_key_value_weight: bfloat16 [4096, 32, 384], P('tok', 'vocab'), may hold values from -0.09375 to 0.09375
- out_weight: bfloat16 [4096, 4096], P('tok', 'vocab'), may hold values from -0.09375 to 0.09375
- dense_weight: bfloat16 [4096, 4096], P('tok', 'vocab'), may hold values from -2 to 2
- head_weight: bfloat16 [4096], P('vocab'), may hold values from -1 to 1
- token_ids: int32 [16, 128], P('tok'), may hold values from 0 to 131071, as said below
- replace_ids: int32 [16, 128], P('tok'), may hold values from 0 to 131071, as said below
- masked: int32 [16, 128], P('tok'), may hold values 0 or 1
- labels: int32 [16, 128], P('tok'), may hold values 0 or 1
- segments: int32 [16, 128], P('tok'), may hold values from 0 to 7, never falling along the last dimension, each value on 1 to 32 neighbouring positions
Outputs:
- table_grads: bfloat16 [131072, 4096], P('tok', 'vocab')
Inputs may be any that keep to these rules, and one draw needn't show every extreme that they name: Ids are split into blocks of 8192 consecutive ids. At every position, token_ids and replace_ids lie in the same block. In each sequence at most 16 positions lie in any one block, and one block holds exactly 16 of them. `replace_ids`: see token_ids.
All inputs are finite; a program needn't handle non-finite values. No bound on the sum of `masked` or of `labels` on one device may be relied on, other than what follows from the above.
Results may differ from a plain program's by a relative error of at most 0.034.
Values may be sent and summed in bfloat16 or wider, within the bound.
A program may use at most 64 MiB of HBM per device.

v0:
```python
import math

import jax
import jax.numpy as jnp
from jax import lax
from jax.sharding import PartitionSpec as P

soft_limit = 50.0
loss_scale = 64.0
epsilon = 1e-05
inv_root_two = 0.7071067811865476
inv_root_tau = 0.3989422804014327


def contract_rows(left_rows, right_rows):
    return lax.dot_general(
        left_rows, right_rows, (((1,), (1,)), ((), ())), preferred_element_type=jnp.float32
    )


def local(
    embeddings,
    norm_gain,
    query_key_value_weight,
    out_weight,
    dense_weight,
    head_weight,
    token_ids,
    replace_ids,
    masked,
    labels,
    segments,
):
    chosen = jnp.where(masked[0] == 1, replace_ids[0], token_ids[0])
    length = chosen.shape[0]
    vocab_rows, columns = embeddings.shape
    tok_count = lax.axis_size("tok")
    full_width = columns * lax.axis_size("vocab")
    heads_here = query_key_value_weight.shape[1]
    head_size = query_key_value_weight.shape[2] // 3
    width_qkv = heads_here * 3 * head_size
    capacity = 2 * length // tok_count
    owner_tokens = chosen // vocab_rows
    offsets = chosen - owner_tokens * vocab_rows
    owner_hot = (owner_tokens[:, None] == jnp.arange(tok_count, dtype=jnp.int32)[None, :]).astype(
        jnp.int32
    )
    slot_index = jnp.sum(owner_hot * (jnp.cumsum(owner_hot, axis=0) - 1), axis=1)
    requests = jnp.zeros((tok_count, capacity), jnp.int32).at[owner_tokens, slot_index].set(offsets)
    fetched = jnp.take(
        embeddings, lax.all_to_all(requests, "tok", split_axis=0, concat_axis=0, tiled=True), axis=0
    )
    replies = lax.all_to_all(fetched, "tok", split_axis=0, concat_axis=0, tiled=True)
    inputs = replies[owner_tokens, slot_index]
    features = inputs.astype(jnp.float32)
    row_sum, row_squares = lax.psum(
        (jnp.sum(features, axis=1), jnp.sum(features * features, axis=1)), "vocab"
    )
    row_mean = row_sum / full_width
    variance = row_squares / full_width - row_mean * row_mean
    inv_std = lax.rsqrt(variance + epsilon)
    centered = (features - row_mean[:, None]) * inv_std[:, None]
    gain = norm_gain.astype(jnp.float32)
    norm_output = (centered * gain[None, :]).astype(jnp.bfloat16)
    panel = lax.all_gather(query_key_value_weight, "tok", axis=0, tiled=True).reshape(
        full_width, width_qkv
    )
    rows_used = panel
    projected = jnp.dot(
        lax.all_gather(norm_output, "vocab", axis=1, tiled=True),
        rows_used,
        preferred_element_type=jnp.float32,
    )
    qkv_parts = projected.astype(jnp.bfloat16).reshape(length, heads_here, 3 * head_size)
    queries = qkv_parts[:, :, :head_size]
    key_rows = qkv_parts[:, :, head_size : 2 * head_size]
    value_rows = qkv_parts[:, :, 2 * head_size :]
    segment_row = segments[0]
    same_segment = segment_row[:, None] == segment_row[None, :]
    raw_scores = jnp.einsum(
        "qhd,khd->hqk", queries, key_rows, preferred_element_type=jnp.float32
    ) / math.sqrt(head_size)
    capped = soft_limit * jnp.tanh(raw_scores / soft_limit)
    exps = jnp.where(same_segment[None], jnp.exp(capped), 0.0)
    probabilities = exps / jnp.sum(exps, axis=-1, keepdims=True)
    prob_rounded = probabilities.astype(jnp.bfloat16)
    head_values = jnp.einsum(
        "hqk,khd->qhd", prob_rounded, value_rows, preferred_element_type=jnp.float32
    )
    head_values = head_values.astype(jnp.bfloat16).reshape(length, heads_here * head_size)
    out_panel, dense_panel = (
        lax.all_gather(out_weight, "tok", axis=0, tiled=True),
        lax.all_gather(dense_weight, "tok", axis=0, tiled=True),
    )
    rows_used = out_panel
    attended = jnp.dot(
        lax.all_gather(head_values, "vocab", axis=1, tiled=True),
        rows_used,
        preferred_element_type=jnp.float32,
    )
    hidden = features + attended
    hidden_narrow = hidden.astype(jnp.bfloat16)
    rows_used = dense_panel
    dense_linear = jnp.dot(
        lax.all_gather(hidden_narrow, "vocab", axis=1, tiled=True),
        rows_used,
        preferred_element_type=jnp.float32,
    )
    activated = jax.nn.gelu(dense_linear, approximate=False)
    activated_sum, activated_squares = lax.psum(
        (jnp.sum(activated, axis=1), jnp.sum(activated * activated, axis=1)), "vocab"
    )
    head_mean = activated_sum / full_width
    head_scale = lax.rsqrt(activated_squares / full_width - head_mean * head_mean + epsilon)
    head_centered = (activated - head_mean[:, None]) * head_scale[:, None]
    head_vector = head_weight.astype(jnp.float32)
    logits = lax.psum(jnp.sum(head_centered * head_vector[None, :], axis=1), "vocab")
    logit_grads = loss_scale * (jax.nn.sigmoid(logits) - labels[0].astype(jnp.float32))
    centered_grads = logit_grads[:, None] * head_vector[None, :]
    gradient_sum, weighted_gradient = lax.psum(
        (jnp.sum(centered_grads, axis=1), jnp.sum(centered_grads * head_centered, axis=1)), "vocab"
    )
    mean_grads = (gradient_sum / full_width)[:, None]
    mean_product = (weighted_gradient / full_width)[:, None]
    activated_grads = head_scale[:, None] * (
        centered_grads - mean_grads - head_centered * mean_product
    )
    gelu_slope = (
        0.5 * (1.0 + lax.erf(dense_linear * inv_root_two))
        + dense_linear * jnp.exp(-0.5 * dense_linear * dense_linear) * inv_root_tau
    )
    pre_grads = (activated_grads * gelu_slope).astype(jnp.bfloat16)
    rows_used = dense_panel
    hidden_grads = (
        lax.psum_scatter(
            contract_rows(rows_used, pre_grads).astype(jnp.bfloat16),
            "vocab",
            scatter_dimension=0,
            tiled=True,
        )
        .astype(jnp.float32)
        .T
    )
    hidden_rounded = hidden_grads.astype(jnp.bfloat16)
    rows_used = out_panel
    out_grads = lax.psum_scatter(
        contract_rows(rows_used, hidden_rounded).astype(jnp.bfloat16),
        "vocab",
        scatter_dimension=0,
        tiled=True,
    ).astype(jnp.float32)
    out_rounded = out_grads.T.astype(jnp.bfloat16).reshape(length, heads_here, head_size)
    prob_grads = jnp.einsum(
        "qhd,khd->hqk", out_rounded, value_rows, preferred_element_type=jnp.float32
    )
    value_grads = jnp.einsum(
        "hqk,qhd->khd", prob_rounded, out_rounded, preferred_element_type=jnp.float32
    )
    capped_grads = probabilities * (
        prob_grads - jnp.sum(probabilities * prob_grads, axis=-1, keepdims=True)
    )
    ratio = capped / soft_limit
    score_grads = capped_grads * (1.0 - ratio * ratio) / math.sqrt(head_size)
    score_rounded = score_grads.astype(jnp.bfloat16)
    query_grads = jnp.einsum(
        "hqk,khd->qhd", score_rounded, key_rows, preferred_element_type=jnp.float32
    )
    key_grads = jnp.einsum(
        "hqk,qhd->khd", score_rounded, queries, preferred_element_type=jnp.float32
    )
    qkv_grads = (
        jnp.concatenate([query_grads, key_grads, value_grads], axis=-1)
        .astype(jnp.bfloat16)
        .reshape(length, width_qkv)
    )
    rows_used = panel
    norm_grads = (
        lax.psum_scatter(
            contract_rows(rows_used, qkv_grads).astype(jnp.bfloat16),
            "vocab",
            scatter_dimension=0,
            tiled=True,
        )
        .astype(jnp.float32)
        .T
    )
    scaled = norm_grads * gain[None, :]
    sum_scaled, sum_weighted = lax.psum(
        (jnp.sum(scaled, axis=1), jnp.sum(scaled * centered, axis=1)), "vocab"
    )
    mean_scaled = (sum_scaled / full_width)[:, None]
    mean_weighted = (sum_weighted / full_width)[:, None]
    input_grads = hidden_grads + inv_std[:, None] * (
        scaled - mean_scaled - centered * mean_weighted
    )
    all_grads, all_chosen = (
        lax.all_gather(input_grads.astype(jnp.bfloat16), "tok", axis=0, tiled=True).astype(
            input_grads.dtype
        ),
        lax.all_gather(chosen, "tok", axis=0, tiled=True),
    )
    local_rows = all_chosen - lax.axis_index("tok") * vocab_rows
    inside = (local_rows >= 0) & (local_rows < vocab_rows)
    row_index = jnp.where(inside, local_rows, 0).astype(jnp.int32)
    contrib = jnp.where(inside[:, None], all_grads, 0.0)
    table_grads = jnp.zeros((vocab_rows, columns), jnp.float32).at[row_index].add(contrib)
    return table_grads.astype(jnp.bfloat16)


def solution(mesh):
    placed = (
        P("tok", "vocab"),
        P("vocab"),
        P("tok", "vocab", None),
        P("tok", "vocab"),
        P("tok", "vocab"),
        P("vocab"),
        P("tok", None),
        P("tok", None),
        P("tok", None),
        P("tok", None),
        P("tok", None),
    )
    return jax.shard_map(
        local, mesh=mesh, in_specs=placed, out_specs=P("tok", "vocab"), check_vma=False
    )
```

profile of v0, /device:TPU:1, one launch (start us, length us, event | category | flops | bytes accessed | tf_op | source)
XLA Modules:
  0.0 1484.0 jit_solution(671828175849446395)
XLA Ops:
  6.5 0.8 bitcast_subtract_fusion.1
  7.9 7.0 scatter_fusion
  14.9 16.3 %all_to_all.20 = s32[16,1,16]{2,1,0:T(1,128)S(1)} all-to-all(s32[16,1,16]{2,1,0:T(1,128)S(1)} %bitcast.130), channel_id=1, replica_groups=mesh['vocab'=32,'tok'=16] {'tok'}, dimensions={0} | all-to-all | bytes 2048 | tf_op jit(solution)/shard_map/all_to_all | solution.py:51
  31.4 0.9 gather_fusion
  32.2 0.7 broadcast_select_fusion
  32.9 4.0 all-to-all-start.1
  36.9 0.7 convert_element_type.88
  37.6 7.1 all-to-all-done.1
  44.7 1.1 gather_fusion.1
  46.0 66.0 %all-reduce.3 = (f32[128]{0:T(128)S(1)}, f32[128]{0:T(128)S(1)}) all-reduce(f32[128]{0:T(128)S(1)} %get-tuple-element.8, f32[128]{0:T(128)S(1)} %get-tuple-element.7), channel_id=1, replica_groups=mesh['vocab'=32,'tok'=16] {'vocab'}, use_global_device_ids=true, to_apply=%region_6.7 | all-reduce | flops 256 | bytes 2048 | tf_op jit(solution)/shard_map/psum | solution.py:56
  112.0 0.7 fusion.42
  112.8 0.7 all-gather.11.cloned.1.call-update
  113.5 0.7 all-gather.13.cloned.1.call-update
  114.3 74.2 %all-gather.9.cloned.1.call-done = bf16[128,4096]{1,0:T(8,128)(2,1)} async-done(((bf16[128,128]{1,0:T(8,128)(2,1)}), bf16[128,4096]{1,0:T(8,128)(2,1)}) %all-gather.9.cloned.1.call-update) | async-done | bytes 1048592 | tf_op jit(solution)/shard_map/all_gather | solution.py:70
  188.5 48.8 %all-gather.11.cloned.1.call-done = bf16[4096,1,384]{2,0,1:T(8,128)(2,1)} async-done(((bf16[256,1,384]{2,0,1:T(8,128)(2,1)}), bf16[4096,1,384]{2,0,1:T(8,128)(2,1)}) %all-gather.11.cloned.1.call-update) | async-done | bytes 3145744 | tf_op jit(solution)/shard_map/all_gather | solution.py:65
  237.3 2.9 fusion.11
  240.3 0.2 fusion.62
  240.5 0.8 fusion.16
  241.4 0.5 all-gather.17.cloned.1.call-update
  241.9 37.2 %all-gather.13.cloned.1.call-done = bf16[4096,128]{1,0:T(8,128)(2,1)} async-done(((bf16[256,128]{1,0:T(8,128)(2,1)}), bf16[4096,128]{1,0:T(8,128)(2,1)}) %all-gather.13.cloned.1.call-update) | async-done | bytes 1048592 | tf_op jit(solution)/shard_map/all_gather | solution.py:92
  279.2 79.5 %all-gather.19.cloned.1.call-done = bf16[128,1,4096]{0,2,1:T(8,128)(2,1)} async-done(((bf16[128,1,128]{0,2,1:T(8,128)(2,1)}), bf16[128,1,4096]{0,2,1:T(8,128)(2,1)}) %all-gather.19.cloned.1.call-update) | async-done | bytes 1048592 | tf_op jit(solution)/shard_map/all_gather | solution.py:97
  358.7 2.6 fusion.15
  361.4 42.2 %all-gather.17.cloned.1.call-done = bf16[4096,128]{1,0:T(8,128)(2,1)} async-done(((bf16[256,128]{1,0:T(8,128)(2,1)}), bf16[4096,128]{1,0:T(8,128)(2,1)}) %all-gather.17.cloned.1.call-update) | async-done | bytes 1048592 | tf_op jit(solution)/shard_map/all_gather | solution.py:93
  403.6 74.7 %all-gather.15.cloned.1.call-done = bf16[128,4096]{1,0:T(8,128)(2,1)} async-done(((bf16[128,128]{1,0:T(8,128)(2,1)}), bf16[128,4096]{1,0:T(8,128)(2,1)}) %all-gather.15.cloned.1.call-update) | async-done | bytes 1048592 | tf_op jit(solution)/shard_map/all_gather | solution.py:105
  478.3 2.2 multiply_reduce_fusion.3
  480.4 59.7 %all-reduce.2 = (f32[128]{0:T(128)S(1)}, f32[128]{0:T(128)S(1)}) all-reduce(f32[128]{0:T(128)S(1)} %get-tuple-element.6, f32[128]{0:T(128)S(1)} %get-tuple-element.5), channel_id=1, replica_groups=mesh['vocab'=32,'tok'=16] {'vocab'}, use_global_device_ids=true, to_apply=%region_11.12 | all-reduce | flops 256 | bytes 2048 | tf_op jit(solution)/shard_map/psum | solution.py:110
  540.2 56.0 %psum.67 = f32[128]{0:T(128)S(1)} all-reduce(f32[128]{0:T(128)S(1)} %multiply_reduce_fusion.2), channel_id=1, replica_groups=mesh['vocab'=32,'tok'=16] {'vocab'}, use_global_device_ids=true, to_apply=%region_13.14 | all-reduce | flops 128 | bytes 1024 | tf_op jit(solution)/shard_map/psum | solution.py:117
  596.4 57.9 %all-reduce.1 = (f32[128]{0:T(128)S(1)}, f32[128]{0:T(128)S(1)}) all-reduce(f32[128]{0:T(128)S(1)} %get-tuple-element.10, f32[128]{0:T(128)S(1)} %get-tuple-element.9), channel_id=1, replica_groups=mesh['vocab'=32,'tok'=16] {'vocab'}, use_global_device_ids=true, to_apply=%region_17.18 | all-reduce | flops 256 | bytes 2048 | tf_op jit(solution)/shard_map/psum | solution.py:120
  654.3 1.8 fusion
  656.1 1.3 copy.13
  657.5 254.2 %reduce-scatter.10.cloned.1.call-done = bf16[128,128]{1,0:T(8,128)(2,1)} async-done(((bf16[4096,128]{1,0:T(8,128)(2,1)}), bf16[128,128]{1,0:T(8,128)(2,1)}) %reduce-scatter.10.cloned.1.call-update) | async-done | bytes 32784
  911.6 1.7 fusion.1
  913.3 1.3 copy.15
  914.7 219.3 %reduce-scatter.12.cloned.1.call-done = bf16[128,128]{1,0:T(8,128)(2,1)} async-done(((bf16[4096,128]{1,0:T(8,128)(2,1)}), bf16[128,128]{1,0:T(8,128)(2,1)}) %reduce-scatter.12.cloned.1.call-update) | async-done | bytes 32784
  1134.0 0.9 multiply_reduce_fusion.1
  1135.1 0.2 fusion.17
  1135.3 0.2 fusion.18
  1135.4 1.0 fusion.19
  1136.4 3.0 fusion.2
  1139.5 1.3 copy.17
  1140.8 22.5 %all-gather = s32[1,2048]{1,0:T(1,128)S(1)} all-gather(s32[1,128]{1,0:T(1,128)S(1)} %get-tuple-element.24), channel_id=2, replica_groups=mesh['vocab'=32,'tok'=16] {'tok'}, dimensions={1}, use_global_device_ids=true | all-gather | bytes 8704 | tf_op jit(solution)/shard_map/all_gather | solution.py:200
  1163.5 195.4 %reduce-scatter.14.cloned.1.call-done = bf16[128,128]{1,0:T(8,128)(2,1)} async-done(((bf16[4096,128]{1,0:T(8,128)(2,1)}), bf16[128,128]{1,0:T(8,128)(2,1)}) %reduce-scatter.14.cloned.1.call-update) | async-done | bytes 32784
  1358.9 0.9 copy.18
  1359.9 0.2 fusion.43
  1360.1 58.4 %all-reduce = (f32[128]{0:T(128)S(1)}, f32[128]{0:T(128)S(1)}) all-reduce(f32[128]{0:T(128)S(1)} %fusion.43, f32[128]{0:T(128)S(1)} %fusion.52), channel_id=1, replica_groups=mesh['vocab'=32,'tok'=16] {'vocab'}, use_global_device_ids=true, to_apply=%region_25.26 | all-reduce | flops 256 | bytes 2048 | tf_op jit(solution)/shard_map/psum | solution.py:188
  1418.7 37.9 %all_gather.31 = bf16[2048,128]{1,0:T(8,128)(2,1)S(1)} all-gather(bf16[128,128]{1,0:T(8,128)(2,1)S(1)} %fusion.47), channel_id=1, replica_groups=mesh['vocab'=32,'tok'=16] {'tok'}, dimensions={0}, use_global_device_ids=true | all-gather | bytes 557056 | tf_op jit(solution)/shard_map/all_gather | solution.py:197
  1456.6 17.2 %scatter_custom_fusion.1 = f32[8192,128]{1,0:T(8,128)} fusion(s32[2048]{0:T(1024)S(1)} %compare_select_fusion.2, f32[]{:T(128)} %constant.47.clone.1, bf16[2048,128]{1,0:T(8,128)(2,1)S(1)} %all_gather.31, pred[2048]{0:T(1024)(128)(4,1)S(1)} %compare_and_fusion.1), kind=kCustom, calls=%fused_computation.13 | custom fusion | flops 786432 | bytes 4721664 | tf_op jit(solution)/shard_map/scatter-add | solution.py:206
  1473.8 3.7 convert_element_type.110
  (52 shorter events, 1.9 us)
Async XLA Ops:
  6.5 24.8 %copy-start = (bf16[8192,128]{1,0:T(8,128)(2,1)S(1)}, bf16[8192,128]{1,0:T(8,128)(2,1)}, u32[]{:S(2)}) copy-start(bf16[8192,128]{1,0:T(8,128)(2,1)} %param.11) | copy-start | bytes 6291460
  14.9 225.3 %copy-start.2 = (s32[1,128]{1,0:T(1,128)S(1)}, s32[1,128]{1,0:T(1,128)}, u32[]{:S(2)}) copy-start(s32[1,128]{1,0:T(1,128)} %param.21) | copy-start | bytes 1540
  32.9 11.8 all-to-all-start.1
  36.9 151.6 %all-gather.9.cloned.1.call-start = ((), (), s32[]{:S(2)}) async-start(), calls=%async_computation.5 | async-start | bytes 1081344 | tf_op jit(solution)/shard_map/all_gather | solution.py:70
  112.7 124.6 %all-gather.11.cloned.1.call-start = ((), (), s32[]{:S(2)}) async-start(), calls=%async_computation.6 | async-start | bytes 3342336 | tf_op jit(solution)/shard_map/all_gather | solution.py:65
  113.5 165.7 %all-gather.13.cloned.1.call-start = ((), (), s32[]{:S(2)}) async-start(), calls=%async_computation.7 | async-start | bytes 1114112 | tf_op jit(solution)/shard_map/all_gather | solution.py:92
  114.2 247.2 %copy-start.3 = (bf16[128]{0:T(256)(128)(2,1)S(1)}, bf16[128]{0:T(256)(128)(2,1)}, u32[]{:S(2)}) copy-start(bf16[128]{0:T(256)(128)(2,1)} %param.16) | copy-start | bytes 772
  114.2 244.5 %all-gather.19.cloned.1.call-start = ((), (), s32[]{:S(2)}) async-start(), calls=%async_computation.10 | async-start | bytes 1081344 | tf_op jit(solution)/shard_map/all_gather | solution.py:97
  240.2 356.0 %copy-start.4 = (s32[1,128]{1,0:T(1,128)S(1)}, s32[1,128]{1,0:T(1,128)}, u32[]{:S(2)}) copy-start(s32[1,128]{1,0:T(1,128)} %param.20) | copy-start | bytes 1540
  241.3 162.3 %all-gather.17.cloned.1.call-start = ((), (), s32[]{:S(2)}) async-start(), calls=%async_computation.9 | async-start | bytes 1114112 | tf_op jit(solution)/shard_map/all_gather | solution.py:93
  241.9 236.4 %all-gather.15.cloned.1.call-start = ((), (), s32[]{:S(2)}) async-start(), calls=%async_computation.8 | async-start | bytes 1081344 | tf_op jit(solution)/shard_map/all_gather | solution.py:105
  361.3 550.3 %reduce-scatter.10.cloned.1.call-start = ((), (), s32[]{:S(2)}) async-start(), calls=%async_computation.11 | async-start | bytes 1081344
  657.4 476.6 %reduce-scatter.12.cloned.1.call-start = ((), (), s32[]{:S(2)}) async-start(), calls=%async_computation.12 | async-start | bytes 1081344
  914.7 444.3 %reduce-scatter.14.cloned.1.call-start = ((), (), s32[]{:S(2)}) async-start(), calls=%async_computation.13 | async-start | bytes 1081344
  1136.4 27.0 %copy-start.1 = (bf16[128,128]{1,0:T(8,128)(2,1)S(1)}, bf16[128,128]{1,0:T(8,128)(2,1)}, u32[]{:S(2)}) copy-start(bf16[128,128]{1,0:T(8,128)(2,1)} %reduce-scatter.10.cloned.1.call-done) | copy-start | bytes 98308
Sparse Core Ops, SparseCore 0:
  112.9 75.5 all-gather.8
  190.6 46.6 all-gather.10
  239.4 39.7 all-gather.12
  282.2 76.4 all-gather.18
  360.6 42.9 all-gather.16
  406.5 71.7 all-gather.14
  657.5 254.0 reduce-scatter.9
  916.0 217.9 reduce-scatter.11
  1140.9 217.9 reduce-scatter.13
where the time goes:
time: 1480 us
  waiting for transfers between devices  1030 us (70%)
  blocking collectives  375 us (25%)
  other arithmetic  25.3 us (2%)
  matrix products  17.5 us (1%)
    unnamed x12, waiting for transfers between devices  671 us
    all_gather x1, waiting for transfers between devices, local(): lax.all_gather(head_values, 'vocab', axis=1, tiled=True)  79.5 us
    all_gather x1, waiting for transfers between devices, local(): lax.all_gather(hidden_narrow, 'vocab', axis=1, tiled=True)  74.7 us
    all_gather x1, waiting for transfers between devices, local(): lax.all_gather(norm_output, 'vocab', axis=1, tiled=True)  74.2 us
    psum x1, blocking collectives, local(): lax.psum((jnp.sum(features, axis=1), jnp.sum(features * features, axis=1)...  66 us
    psum x1, blocking collectives, local(): lax.psum((jnp.sum(activated, axis=1), jnp.sum(activated * activated, axis...  59.7 us
    psum x1, blocking collectives, local(): lax.psum((jnp.sum(scaled, axis=1), jnp.sum(scaled * centered, axis=1)), '...  58.4 us
    psum x1, blocking collectives, local(): lax.psum((jnp.sum(centered_grads, axis=1), jnp.sum(centered_grads * head_...  57.9 us
  transfers between devices with their start and end apart: 10, of which 10 were waited for; matrix products, arithmetic and copies ran while one was open for 0% of the time, Pallas kernels for 0%

commit v1 on v0

v1 whole, which is shorter than its diff:
```python
import functools
import math

import jax
import jax.numpy as jnp
from jax import lax
from jax.experimental import pallas as pl
from jax.experimental.pallas import tpu as pltpu
from jax.sharding import PartitionSpec as P

MESH = pl.DeviceIdType.MESH
BF = jnp.bfloat16
F32 = jnp.float32
B = 128

soft_limit = 50.0
loss_scale = 64.0
epsilon = 1e-05
inv_root_two = 0.7071067811865476
inv_root_tau = 0.3989422804014327


def dot(a, b):
    return jnp.dot(a, b, preferred_element_type=F32)


def dot_nt(a, b):
    return lax.dot_general(a, b, (((1,), (1,)), ((), ())), preferred_element_type=F32)


def dot_tn(a, b):
    return lax.dot_general(a, b, (((0,), (0,)), ((), ())), preferred_element_type=F32)


def iota(shape, dim):
    return lax.broadcasted_iota(jnp.int32, shape, dim)


def columns_to_rows(columns):
    lane = iota((B, B), 1)
    total = jnp.zeros((B, B), F32)
    for i, column in enumerate(columns):
        total = jnp.where(lane == i, column, total)
    return total.T[:8]


def rows_to_square(rows):
    return jnp.concatenate([rows, jnp.zeros((B - 8, B), F32)], axis=0).T


def row_to_square(row):
    return jnp.broadcast_to(row, (B, B)).T


def main_kernel(
    X, Z, Y, C, vocab_rows,
    emb_hbm, gain_ref, wq_ref, wo_ref, wd_ref, hw_ref,
    tok_ref, rep_ref, mask_ref, lab_ref, seg_ref,
    grad_out, req_out,
    emb, wod_src, Wq, Wod,
    ids_src, ids_buf, row_src, row_buf, gslot_src, gslot_buf,
    x_src, x_buf, h_src, h_buf, d_src, d_buf,
    pq, pq_buf, po, po_buf, pd, pd_buf,
    pre_buf, b1, b1_buf, hr_buf, b2, b2_buf, g_buf, b3, b3_buf,
    nrm, ar_src, ar_buf,
    emb_sem, w1q_sem, w1o_sem, w1_send, w2_recv, w2_send, sib_recv, sib_send,
    t_recv, t_send, e_recv, e_send, e0_send, rx_recv, rx_send, ax_recv, ax_send,
    r_recv, r_send, s_recv, s_send,
):
    V, T = X * Z, Y * C
    Xc = X // C
    D = V * B
    K = Z * B
    v, t = lax.axis_index("vocab"), lax.axis_index("tok")
    x, z = v // Z, v % Z
    y, c = t // C, t % C
    cap = 2 * B // T
    R = T * cap

    def dev(xx, zz, yy, cc):
        return (xx * Z + zz, yy * C + cc)

    def remote(src, dst, send, recv, device):
        return pltpu.make_async_remote_copy(
            src_ref=src, dst_ref=dst, send_sem=send, recv_sem=recv,
            device_id=device, device_id_type=MESH,
        )

    def wait_bytes(ref, sem):
        pltpu.make_async_copy(ref, ref, sem).wait()

    emb_copy = pltpu.make_async_copy(emb_hbm, emb, emb_sem)
    emb_copy.start()
    barrier = pltpu.get_barrier_semaphore()

    def greet_vocab(d, carry):
        pl.semaphore_signal(barrier, inc=1, device_id=((v + d) % V, t), device_id_type=MESH)
        return carry

    def greet_tok(d, carry):
        pl.semaphore_signal(barrier, inc=1, device_id=(v, (t + d) % T), device_id_type=MESH)
        return carry

    lax.fori_loop(1, V, greet_vocab, 0)
    lax.fori_loop(1, T, greet_tok, 0)
    same_core = (x // Xc) == c

    @pl.when(jnp.logical_not(same_core))
    def _():
        for i in range(Xc):
            pl.semaphore_signal(
                barrier, inc=1, device_id=dev(Xc * c + i, z, y, x // Xc), device_id_type=MESH
            )

    wod_src[:, 0:B] = wo_ref[...]
    wod_src[:, B : 2 * B] = wd_ref[...]
    chosen = jnp.where(mask_ref[...] == 1, rep_ref[...], tok_ref[...])
    owner = chosen // vocab_rows
    offset = (chosen - owner * vocab_rows).astype(F32)
    owner_f = owner.astype(F32)
    earlier = iota((B, B), 0) < iota((B, B), 1)
    same_owner = row_to_square(owner_f) == owner_f
    slot = jnp.sum(jnp.where(same_owner & earlier, 1.0, 0.0), axis=0, keepdims=True)
    place = owner_f * float(cap) + slot
    place_hot = iota((R, B), 0).astype(F32) == place
    wanted = jnp.sum(jnp.where(place_hot, offset, 0.0), axis=1, keepdims=True)
    ids_src[...] = jnp.broadcast_to(wanted, (R, B)).reshape(T, cap, B)
    put_hot = jnp.where(place_hot, 1.0, 0.0).astype(BF)

    peers = V - 1 + T - 1

    @pl.when(same_core)
    def _():
        pl.semaphore_wait(barrier, peers)

    @pl.when(jnp.logical_not(same_core))
    def _():
        pl.semaphore_wait(barrier, peers + Xc)

    def tok_start(src, buf, n):
        buf[t] = src[t]

        def send(d, carry):
            to = (t + d) % T
            remote(src.at[to], buf.at[t], t_send.at[n], t_recv.at[n], (v, to)).start()
            return carry

        lax.fori_loop(1, T, send, 0)

    def tok_wait(src, buf, n):
        wait_bytes(buf.at[pl.ds(0, T - 1)], t_recv.at[n])

    def tok_done(src, buf, n):
        wait_bytes(src.at[pl.ds(0, T - 1)], t_send.at[n])

    tok_start(ids_src, ids_buf, 0)

    def w1_each(act):
        for i in range(Xc):
            xd, cd = Xc * c + i, x // Xc
            mine = (xd == x) & same_core
            rows = pl.ds(i * B, B)
            dst_rows = pl.ds(pl.multiple_of(y * B, B), B)
            q = (wq_ref.at[rows], Wq.at[x, dst_rows], w1q_sem)
            o = (wod_src.at[rows], Wod.at[x, dst_rows], w1o_sem)
            for a, (src, dst, sem) in enumerate((q, o)):
                act(mine, src, dst, sem, w1_send.at[i, a], dev(xd, z, y, cd))

    def w1_go(mine, src, dst, sem, send, device):
        @pl.when(mine)
        def _():
            pltpu.make_async_copy(src, dst, sem).start()

        @pl.when(jnp.logical_not(mine))
        def _():
            remote(src, dst, send, sem, device).start()

    def w1_end(mine, src, dst, sem, send, device):
        @pl.when(jnp.logical_not(mine))
        def _():
            wait_bytes(src, send)

    w1_each(w1_go)

    arrays = (Wq, Wod)
    right_hops, left_hops = Y // 2, Y - 1 - Y // 2

    def slab(a, k):
        return arrays[a].at[pl.ds(Xc * c, Xc), pl.ds(pl.multiple_of(k * B, B), B)]

    def hop(a, h, way):
        step = 1 if way == 0 else Y - 1
        k = (y + (Y - step) * (h - 1)) % Y
        ref = slab(a, k)
        return remote(
            ref, ref, w2_send.at[a, way, h - 1], w2_recv.at[a, way, h - 1],
            dev(x, z, (y + step) % Y, c),
        )

    def sibling(a, k, n):
        ref = slab(a, k)
        return remote(ref, ref, sib_send.at[a, n], sib_recv.at[a, n], dev(x, z, y, (c + 1) % C))

    def hops_of(way):
        return right_hops if way == 0 else left_hops

    def arrived(h, way):
        step = 1 if way == 0 else Y - 1
        return (y + (Y - step) * h) % Y

    def w2_begin(a):
        wait_bytes(arrays[a].at[pl.ds(0, Xc), pl.ds(0, B)], (w1q_sem, w1o_sem)[a])
        for way in (0, 1):
            if hops_of(way) >= 1:
                hop(a, 1, way).start()
        sibling(a, y, 0).start()

    def sib_slot(h, way):
        return h if way == 0 else right_hops + h

    def w2_forward(a, h):
        for way in (0, 1):
            if h <= hops_of(way):
                hop(a, h, way).wait_recv()
                if h + 1 <= hops_of(way):
                    hop(a, h + 1, way).start()
                sibling(a, arrived(h, way), sib_slot(h, way)).start()

    def w2_ready(a):
        for n in range(Y):
            wait_bytes(arrays[a].at[pl.ds(0, Xc), pl.ds(0, B)], sib_recv.at[a, n])

    def w2_done(a):
        for way in (0, 1):
            for h in range(1, hops_of(way) + 1):
                hop(a, h, way).wait_send()
        for n in range(Y):
            wait_bytes(arrays[a].at[pl.ds(0, Xc), pl.ds(0, B)], sib_send.at[a, n])

    row = z % X
    at_home = x == row

    def row_start(src, buf, n):
        k = v // X
        for j in list(range(1, Z)):
            remote(src, buf.at[k], e_send.at[n], e_recv.at[n], dev(row, (z + j) % Z, y, c)).start()

        @pl.when(at_home)
        def _():
            pltpu.make_async_copy(src, buf.at[k], e_recv.at[n]).start()

        @pl.when(jnp.logical_not(at_home))
        def _():
            remote(src, buf.at[k], e0_send.at[n], e_recv.at[n], dev(row, z, y, c)).start()

    def row_wait(src, buf, n):
        wait_bytes(buf, e_recv.at[n])

    def row_done(src, buf, n):
        wait_bytes(buf.at[pl.ds(0, Z - 1)], e_send.at[n])

        @pl.when(jnp.logical_not(at_home))
        def _():
            wait_bytes(src, e0_send.at[n])

    def rx_start(part, buf, n):
        for d in range(1, X):
            to = (x + d) % X
            remote(
                part.at[to], buf.at[d - 1], rx_send.at[n], rx_recv.at[n], dev(to, z, y, c)
            ).start()

    def rx_sum(part, buf, n):
        wait_bytes(buf, rx_recv.at[n])
        total = part[x].astype(F32)
        for d in range(1, X):
            total = total + buf[d - 1].astype(F32)
        return total

    def ax_start(buf, n):
        for d in range(1, X):
            remote(
                buf.at[x], buf.at[x], ax_send.at[n], ax_recv.at[n], dev((x + d) % X, z, y, c)
            ).start()

    def ax_wait(buf, n):
        wait_bytes(buf.at[pl.ds(0, X - 1)], ax_recv.at[n])

    def own_start(part, buf, k, n):
        to = X * k + x
        mine = to == v

        @pl.when(mine)
        def _():
            pltpu.make_async_copy(part.at[k], buf.at[z], r_recv.at[n]).start()

        @pl.when(jnp.logical_not(mine))
        def _():
            remote(part.at[k], buf.at[z], r_send.at[n, k], r_recv.at[n], (to, t)).start()

    def own_sum(buf, n):
        wait_bytes(buf, r_recv.at[n])
        total = buf[0].astype(F32)
        for k in range(1, Z):
            total = total + buf[k].astype(F32)
        return total

    def own_done(part, n):
        for k in range(Z):
            @pl.when(X * k + x != v)
            def _():
                wait_bytes(part.at[k], r_send.at[n, k])

    def spread_back(left, weights, part, buf, n):
        step = 2
        for first in range(0, Z, step):
            total = None
            for xx in range(X):
                term = dot_nt(left(xx), weights(xx, pl.ds(first * B, step * B)))
                total = term if total is None else total + term
            for k in range(first, first + step):
                part[k] = total[:, (k - first) * B : (k - first + 1) * B].astype(BF)
                own_start(part, buf, k, n)

    def ar_start(rows, n):
        ar_src[n] = rows
        ar_buf[n, 0] = rows

        def send(d, carry):
            remote(
                ar_src.at[n], ar_buf.at[n, d], s_send.at[n], s_recv.at[n], ((v + d) % V, t)
            ).start()
            return carry

        lax.fori_loop(1, V, send, 0)

    def ar_sum(n):
        wait_bytes(ar_buf.at[n, pl.ds(1, V - 1)], s_recv.at[n])
        return rows_to_square(jnp.sum(ar_buf[n], axis=0))

    def ar_done(n):
        wait_bytes(ar_buf.at[n, pl.ds(1, V - 1)], s_send.at[n])

    place_square = row_to_square(place)
    take_hot = jnp.concatenate(
        [
            jnp.where(place_square == (iota((B, B), 1) + first).astype(F32), 1.0, 0.0)
            for first in range(0, R, B)
        ],
        axis=1,
    ).astype(BF)
    emb_copy.wait()
    tok_wait(ids_src, ids_buf, 0)
    requested = ids_buf[...].reshape(R, B)
    chunk = 512

    def fetch(i, total):
        base = i * chunk
        hot = jnp.concatenate(
            [
                jnp.where(
                    requested == (iota((R, B), 1) + (base + first)).astype(F32), 1.0, 0.0
                ).astype(BF)
                for first in range(0, chunk, B)
            ],
            axis=1,
        )
        return total + dot(hot, emb[pl.ds(pl.multiple_of(base, chunk), chunk), :])

    fetched = lax.fori_loop(0, vocab_rows // chunk, fetch, jnp.zeros((R, B), F32))
    row_src[...] = fetched.astype(BF).reshape(T, cap, B)
    tok_start(row_src, row_buf, 1)
    w2_begin(0)
    for first in range(0, R, B):
        req_out[:, first : first + B] = requested[first : first + B].T[:8]
    w2_forward(0, 1)
    tok_wait(row_src, row_buf, 1)
    inputs = dot(take_hot, row_buf[...].reshape(R, B))
    features = inputs
    gain = gain_ref[...].astype(F32)
    x_src[0:B, :] = inputs.astype(BF)
    x_src[B : B + 16, :] = jnp.broadcast_to(gain_ref[...].astype(F32), (16, B)).astype(BF)
    row_start(x_src, x_buf, 0)
    ar_start(
        columns_to_rows(
            [
                jnp.sum(features, axis=1, keepdims=True),
                jnp.sum(features * features, axis=1, keepdims=True),
            ]
        ),
        0,
    )
    w2_forward(0, 2)
    stats = ar_sum(0)
    row_mean = stats[:, 0:1] / D
    variance = stats[:, 1:2] / D - row_mean * row_mean
    inv_std = lax.rsqrt(variance + epsilon)
    centered = (features - row_mean) * inv_std
    w2_forward(0, 3)
    row_wait(x_src, x_buf, 0)
    for k in range(Z):
        block = x_buf[k, 0:B, :].astype(F32)
        block_gain = x_buf[k, B : B + 16, :].astype(F32)[0:1]
        nrm[:, k * B : (k + 1) * B] = (((block - row_mean) * inv_std) * block_gain).astype(BF)
    w2_forward(0, 4)
    w2_begin(1)
    w2_ready(0)

    for xx in range(X):
        pq[xx] = dot(nrm[...], Wq[xx]).astype(BF)
    rx_start(pq, pq_buf, 0)
    w2_forward(1, 1)
    qkv = rx_sum(pq, pq_buf, 0).astype(BF)
    queries, keys, values = qkv[:, :B], qkv[:, B : 2 * B], qkv[:, 2 * B :]
    segment_f = seg_ref[...].astype(F32)
    same_segment = row_to_square(segment_f) == segment_f
    raw = dot_nt(queries, keys) / math.sqrt(B)
    capped = soft_limit * jnp.tanh(raw / soft_limit)
    exps = jnp.where(same_segment, jnp.exp(capped), 0.0)
    probabilities = exps / jnp.sum(exps, axis=-1, keepdims=True)
    prob_rounded = probabilities.astype(BF)
    h_src[...] = dot(prob_rounded, values).astype(BF)
    row_start(h_src, h_buf, 1)
    w2_forward(1, 2)
    w2_forward(1, 3)
    w2_forward(1, 4)
    row_wait(h_src, h_buf, 1)
    w2_ready(1)

    heads_row = jnp.concatenate([h_buf[k] for k in range(Z)], axis=1)
    for xx in range(X):
        po[xx] = dot(heads_row, Wod[xx, :, 0:B]).astype(po.dtype)
    rx_start(po, po_buf, 1)
    hidden = features + rx_sum(po, po_buf, 1)
    d_src[...] = hidden.astype(BF)
    row_start(d_src, d_buf, 2)
    row_wait(d_src, d_buf, 2)

    dense_row = jnp.concatenate([d_buf[k] for k in range(Z)], axis=1)
    for xx in range(X):
        pd[xx] = dot(dense_row, Wod[xx, :, B : 2 * B]).astype(pd.dtype)
    rx_start(pd, pd_buf, 2)
    dense_linear = rx_sum(pd, pd_buf, 2)
    phi = 0.5 * (1.0 + lax.erf(dense_linear * inv_root_two))
    activated = dense_linear * phi
    head_vector = hw_ref[...].astype(F32)
    ar_start(
        columns_to_rows(
            [
                jnp.sum(activated, axis=1, keepdims=True),
                jnp.sum(activated * activated, axis=1, keepdims=True),
                jnp.sum(activated * head_vector, axis=1, keepdims=True),
                jnp.broadcast_to(jnp.sum(head_vector, axis=1, keepdims=True), (B, 1)),
            ]
        ),
        1,
    )
    gelu_slope = phi + dense_linear * jnp.exp(-0.5 * dense_linear * dense_linear) * inv_root_tau
    labels = row_to_square(lab_ref[...].astype(F32))[:, 0:1]
    stats = ar_sum(1)
    head_mean = stats[:, 0:1] / D
    head_scale = lax.rsqrt(stats[:, 1:2] / D - head_mean * head_mean + epsilon)
    weight_sum = stats[:, 3:4]
    logits = head_scale * (stats[:, 2:3] - head_mean * weight_sum)
    logit_grads = loss_scale * (jax.nn.sigmoid(logits) - labels)
    head_centered = (activated - head_mean) * head_scale
    mean_grads = logit_grads * weight_sum / D
    mean_product = logit_grads * logits / D
    activated_grads = head_scale * (
        logit_grads * head_vector - mean_grads - head_centered * mean_product
    )
    pre_buf[x] = (activated_grads * gelu_slope).astype(BF)
    ax_start(pre_buf, 0)
    ax_wait(pre_buf, 0)
    spread_back(
        lambda xx: pre_buf[xx], lambda xx, rows: Wod[xx, rows, B : 2 * B], b1, b1_buf, 0
    )
    hidden_grads = own_sum(b1_buf, 0)
    hr_buf[x] = hidden_grads.astype(BF)
    ax_start(hr_buf, 1)
    ax_wait(hr_buf, 1)
    spread_back(lambda xx: hr_buf[xx], lambda xx, rows: Wod[xx, rows, 0:B], b2, b2_buf, 1)
    out_rounded = own_sum(b2_buf, 1).astype(BF)

    prob_grads = dot_nt(out_rounded, values)
    value_grads = dot_tn(prob_rounded, out_rounded)
    capped_grads = probabilities * (
        prob_grads - jnp.sum(probabilities * prob_grads, axis=-1, keepdims=True)
    )
    ratio = capped / soft_limit
    score_rounded = (capped_grads * (1.0 - ratio * ratio) / math.sqrt(B)).astype(BF)
    query_grads = dot(score_rounded, keys)
    key_grads = dot_tn(score_rounded, queries)
    g_buf[x] = jnp.concatenate([query_grads, key_grads, value_grads], axis=1).astype(BF)
    ax_start(g_buf, 2)
    ax_wait(g_buf, 2)
    spread_back(lambda xx: g_buf[xx], lambda xx, rows: Wq[xx, rows, :], b3, b3_buf, 2)
    scaled = own_sum(b3_buf, 2) * gain
    ar_start(
        columns_to_rows(
            [
                jnp.sum(scaled, axis=1, keepdims=True),
                jnp.sum(scaled * centered, axis=1, keepdims=True),
            ]
        ),
        2,
    )
    stats = ar_sum(2)
    input_grads = hidden_grads + inv_std * (
        scaled - stats[:, 0:1] / D - centered * (stats[:, 1:2] / D)
    )

    gslot_src[...] = dot(put_hot, input_grads.astype(BF)).astype(BF).reshape(T, cap, B)
    tok_start(gslot_src, gslot_buf, 2)
    tok_wait(gslot_src, gslot_buf, 2)
    grad_out[...] = gslot_buf[...].reshape(R, B)

    tok_done(ids_src, ids_buf, 0)
    tok_done(row_src, row_buf, 1)
    tok_done(gslot_src, gslot_buf, 2)
    w1_each(w1_end)
    w2_done(0)
    w2_done(1)
    row_done(x_src, x_buf, 0)
    row_done(h_src, h_buf, 1)
    row_done(d_src, d_buf, 2)
    for n, buf in enumerate((pq_buf, po_buf, pd_buf)):
        wait_bytes(buf, rx_send.at[n])
    for n, buf in enumerate((pre_buf, hr_buf, g_buf)):
        wait_bytes(buf.at[pl.ds(0, X - 1)], ax_send.at[n])
    for n, part in enumerate((b1, b2, b3)):
        own_done(part, n)
    for n in range(3):
        ar_done(n)


def table_kernel(tile, grad_ref, req_ref, out_ref):
    base = pl.program_id(0) * tile
    hot = jnp.where(
        (iota((tile, req_ref.shape[1]), 0) + base).astype(F32) == req_ref[0:1, :], 1.0, 0.0
    ).astype(BF)
    out_ref[...] = dot(hot, grad_ref[...]).astype(BF)


def local(
    X, Z, Y, C,
    embeddings, norm_gain, query_key_value_weight, out_weight, dense_weight, head_weight,
    token_ids, replace_ids, masked, labels, segments,
):
    vocab_rows = embeddings.shape[0]
    V, T = X * Z, Y * C
    cap = 2 * B // T
    R = T * cap
    vm = pl.BlockSpec(memory_space=pltpu.VMEM)
    dma = pltpu.SemaphoreType.DMA
    rows = query_key_value_weight.shape[0]
    VM = pltpu.VMEM
    right = Y // 2
    grads, requests = pl.pallas_call(
        functools.partial(main_kernel, X, Z, Y, C, vocab_rows),
        out_shape=(
            jax.ShapeDtypeStruct((R, B), BF),
            jax.ShapeDtypeStruct((8, R), F32),
        ),
        in_specs=[pl.BlockSpec(memory_space=pl.ANY)] + [vm] * 10,
        out_specs=(vm, vm),
        scratch_shapes=[
            VM((vocab_rows, B), BF),
            VM((rows, 2 * B), BF),
            VM((X, Z * B, 3 * B), BF),
            VM((X, Z * B, 2 * B), BF),
            VM((T, cap, B), F32), VM((T, cap, B), F32),
            VM((T, cap, B), BF), VM((T, cap, B), BF),
            VM((T, cap, B), BF), VM((T, cap, B), BF),
            VM((B + 16, B), BF), VM((Z, B + 16, B), BF),
            VM((B, B), BF), VM((Z, B, B), BF),
            VM((B, B), BF), VM((Z, B, B), BF),
            VM((X, B, 3 * B), BF), VM((X - 1, B, 3 * B), BF),
            VM((X, B, B), F32), VM((X - 1, B, B), F32),
            VM((X, B, B), F32), VM((X - 1, B, B), F32),
            VM((X, B, B), BF), VM((Z, B, B), BF), VM((Z, B, B), BF),
            VM((X, B, B), BF), VM((Z, B, B), BF), VM((Z, B, B), BF),
            VM((X, B, 3 * B), BF), VM((Z, B, B), BF), VM((Z, B, B), BF),
            VM((B, Z * B), BF),
            VM((3, 8, B), F32), VM((3, V, 8, B), F32),
            dma(()), dma(()), dma(()), dma((X // C, 2)),
            dma((2, 2, right)), dma((2, 2, right)), dma((2, Y)), dma((2, Y)),
            dma((3,)), dma((3,)), dma((3,)), dma((3,)), dma((3,)),
            dma((3,)), dma((3,)), dma((3,)), dma((3,)),
            dma((3,)), dma((3, Z)), dma((3,)), dma((3,)),
        ],
        compiler_params=pltpu.CompilerParams(
            collective_id=0, has_side_effects=True, vmem_limit_bytes=40 * 1024 * 1024
        ),
    )(
        embeddings,
        norm_gain.reshape(1, B),
        query_key_value_weight.reshape(rows, 3 * B),
        out_weight,
        dense_weight,
        head_weight.reshape(1, B),
        token_ids, replace_ids, masked, labels, segments,
    )
    tile = min(1024, vocab_rows)
    return pl.pallas_call(
        functools.partial(table_kernel, tile),
        grid=(vocab_rows // tile,),
        out_shape=jax.ShapeDtypeStruct((vocab_rows, B), BF),
        in_specs=[
            pl.BlockSpec((R, B), lambda i: (0, 0)),
            pl.BlockSpec((8, R), lambda i: (0, 0)),
        ],
        out_specs=pl.BlockSpec((tile, B), lambda i: (i, 0)),
    )(grads, requests)


def solution(mesh):
    V, T = mesh.shape["vocab"], mesh.shape["tok"]
    X = 4 if V == 32 else 2
    C = 2
    placed = (
        P("tok", "vocab"),
        P("vocab"),
        P("tok", "vocab", None),
        P("tok", "vocab"),
        P("tok", "vocab"),
        P("vocab"),
        P("tok", None),
        P("tok", None),
        P("tok", None),
        P("tok", None),
        P("tok", None),
    )
    return jax.shard_map(
        functools.partial(local, X, V // X, T // C, C),
        mesh=mesh, in_specs=placed, out_specs=P("tok", "vocab"), check_vma=False,
    )
```

time: 1480 us -> 188 us (0.13)
  waiting for transfers between devices: 1030 us -> 0 us
  blocking collectives: 375 us -> 0 us
  Pallas kernels: 0 us -> 178 us
  other arithmetic: 25.3 us -> 0 us
  matrix products: 17.5 us -> 0 us
    unnamed x12 -> x0, waiting for transfers between devices: 671 us -> none
    all_gather x6 -> x0, waiting for transfers between devices: 357 us -> none  [the longest x1 79.5 us: local(): lax.all_gather(head_values, 'vocab', axis=1, tiled=True)]
    psum x5 -> x0, blocking collectives: 298 us -> none  [the longest x1 66 us: local(): lax.psum((jnp.sum(features, axis=1), jnp.sum(features * features, axis=1)...]
    pallas_call x0 -> x2, Pallas kernels: none -> 178 us  [the longest x1 173 us: local(): pl.pallas_call(functools.partial(main_kernel, X, Z, Y, C, vocab_rows), ou...]
    all_gather x2 -> x0, blocking collectives: 60.4 us -> none  [the longest x1 37.9 us: local(): lax.all_gather(input_grads.astype(jnp.bfloat16), 'tok', axis=0, tiled=True)]
    dot_general x12 -> x0, matrix products: 17.5 us -> none  [the longest x3 6.48 us: contract_rows(): lax.dot_general(left_rows, right_rows, (((1,), (1,)), ((), ())), preferre...]
    scatter-add x1 -> x0, other arithmetic: 17.2 us -> none  [local(): jnp.zeros((vocab_rows, columns), jnp.float32).at[row_index].add(contrib)]
    all_to_all x1 -> x0, blocking collectives: 16.3 us -> none  [local(): lax.all_to_all(requests, 'tok', split_axis=0, concat_axis=0, tiled=True)]
  transfers between devices with their start and end apart: 10 -> 0, of which waited for: 10 -> 0; matrix products, arithmetic and copies ran while one was open for 0% -> 0% of each run, Pallas kernels for 0% -> 0%
where the time goes in v1:
time: 188 us
  Pallas kernels  178 us (95%)
  local copies, waits for them, and re-layouts  10 us (5%)
    pallas_call x1, Pallas kernels, local(): pl.pallas_call(functools.partial(main_kernel, X, Z, Y, C, vocab_rows), ou...  173 us
    unnamed x26, local copies, waits for them, and re-layouts  10 us
    pallas_call x1, Pallas kernels, local(): pl.pallas_call(functools.partial(table_kernel, tile), grid=(vocab_rows //...  5.18 us

profile of v1, /device:TPU:1, one launch (start us, length us, event | category | flops | bytes accessed | tf_op | source)
XLA Modules:
  0.0 187.8 jit_solution(5484339222183476542)
XLA Ops:
  0.0 0.0 copy-start
  0.0 1.6 copy-done
  1.6 0.0 copy-start.1
  1.6 0.9 copy-done.1
  2.5 0.0 copy-start.2
  2.5 0.8 copy-done.2
  3.4 0.0 copy-start.3
  3.4 0.8 copy-done.3
  4.2 0.0 copy-start.6
  4.2 0.7 copy-done.6
  4.9 0.0 copy-start.7
  4.9 0.7 copy-done.7
  5.5 0.0 copy-start.8
  5.5 0.7 copy-done.8
  6.2 0.0 copy-start.9
  6.2 0.7 copy-done.9
  6.8 0.0 copy-start.10
  6.8 0.7 copy-done.10
  7.5 0.0 copy-start.11
  7.5 0.7 copy-done.11
  8.1 0.0 copy-start.12
  8.1 0.7 copy-done.12
  8.8 172.6 %shard_map.109 = (bf16[256,128]{1,0:T(8,128)(2,1)S(1)}, f32[8,256]{1,0:T(8,128)S(1)}) custom-call(bf16[8192,128]{1,0:T(8,128)(2,1)S(1)} %copy-done, bf16[1,128]{1,0:T(2,128)(2,1)S(1)} %bitcast.4, bf16[256,384]{1,0:T(8,128)(2,1)S(1)} %bitcast.3, bf16[256,128]{1,0:T(8,128)(2,1)S(1)} %copy-done.2, bf16[256,128]{1,0:T(8,128)(2,1)S(1)} %copy-done.3, ...), custom_call_target="tpu_custom_call" | custom-call | tf_op jit(solution)/shard_map/pallas_call | solution.py:559
  181.4 0.0 copy-start.4
  181.4 0.6 copy-done.4
  182.0 0.0 copy-start.5
  182.0 0.6 copy-done.5
  182.6 5.2 %shard_map.110 = bf16[8192,128]{1,0:T(8,128)(2,1)} custom-call(bf16[256,128]{1,0:T(8,128)(2,1)} %copy-done.4, f32[8,256]{1,0:T(8,128)} %copy-done.5), custom_call_target="tpu_custom_call" | custom-call | tf_op jit(solution)/shard_map/pallas_call | solution.py:605
Async XLA Ops:
  0.0 1.6 copy-start
  1.6 0.9 copy-start.1
  2.5 0.8 copy-start.2
  3.4 0.8 copy-start.3
  4.2 0.7 copy-start.6
  4.9 0.7 copy-start.7
  5.5 0.7 copy-start.8
  6.2 0.7 copy-start.9
  6.8 0.7 copy-start.10
  7.5 0.7 copy-start.11
  8.1 0.7 copy-start.12
  181.4 0.6 copy-start.4
  182.0 0.6 copy-start.5

commit v2 on v1

--- a/solution.py
+++ b/solution.py
@@ -54,16 +54,17 @@
 
 def main_kernel(
     X, Z, Y, C, vocab_rows,
-    emb_hbm, gain_ref, wq_ref, wo_ref, wd_ref, hw_ref,
-    tok_ref, rep_ref, mask_ref, lab_ref, seg_ref,
+    emb_hbm, gain_hbm, wq_hbm, wo_hbm, wd_hbm, hw_hbm,
+    tok_hbm, rep_hbm, mask_hbm, lab_hbm, seg_hbm,
     grad_out, req_out,
-    emb, wod_src, Wq, Wod,
+    emb, wq_ref, wod_src, Wq, Wod,
+    tok_ref, rep_ref, mask_ref, gain_ref, hw_ref, lab_ref, seg_ref,
     ids_src, ids_buf, row_src, row_buf, gslot_src, gslot_buf,
     x_src, x_buf, h_src, h_buf, d_src, d_buf,
     pq, pq_buf, po, po_buf, pd, pd_buf,
-    pre_buf, b1, b1_buf, hr_buf, b2, b2_buf, g_buf, b3, b3_buf,
-    nrm, ar_src, ar_buf,
-    emb_sem, w1q_sem, w1o_sem, w1_send, w2_recv, w2_send, sib_recv, sib_send,
+    b1, b1_buf, hr_buf, b2, b2_buf, g_buf, b3, b3_buf,
+    nrm, cgain, gains, dl_buf, pre, hw_buf, ar_src, ar_buf,
+    in_sem, w1q_sem, w1o_sem, w1_send, w2_recv, w2_send, sib_recv, sib_send,
     t_recv, t_send, e_recv, e_send, e0_send, rx_recv, rx_send, ax_recv, ax_send,
     r_recv, r_send, s_recv, s_send,
 ):
@@ -86,11 +87,26 @@
             device_id=device, device_id_type=MESH,
         )
 
+    pending = []
+
+    def finish():
+        for done in pending:
+            done()
+
     def wait_bytes(ref, sem):
         pltpu.make_async_copy(ref, ref, sem).wait()
 
-    emb_copy = pltpu.make_async_copy(emb_hbm, emb, emb_sem)
-    emb_copy.start()
+    wanted_here = (
+        (tok_hbm, tok_ref), (rep_hbm, rep_ref), (mask_hbm, mask_ref),
+        (wq_hbm, wq_ref), (wo_hbm, wod_src.at[:, pl.ds(0, B)]),
+        (wd_hbm, wod_src.at[:, pl.ds(B, B)]), (emb_hbm, emb),
+        (gain_hbm, gain_ref), (hw_hbm, hw_ref), (lab_hbm, lab_ref), (seg_hbm, seg_ref),
+    )
+    copies = [
+        pltpu.make_async_copy(src, dst, in_sem.at[i]) for i, (src, dst) in enumerate(wanted_here)
+    ]
+    for copy in copies:
+        copy.start()
     barrier = pltpu.get_barrier_semaphore()
 
     def greet_vocab(d, carry):
@@ -112,8 +128,8 @@
                 barrier, inc=1, device_id=dev(Xc * c + i, z, y, x // Xc), device_id_type=MESH
             )
 
-    wod_src[:, 0:B] = wo_ref[...]
-    wod_src[:, B : 2 * B] = wd_ref[...]
+    for copy in copies[:3]:
+        copy.wait()
     chosen = jnp.where(mask_ref[...] == 1, rep_ref[...], tok_ref[...])
     owner = chosen // vocab_rows
     offset = (chosen - owner * vocab_rows).astype(F32)
@@ -125,7 +141,8 @@
     place_hot = iota((R, B), 0).astype(F32) == place
     wanted = jnp.sum(jnp.where(place_hot, offset, 0.0), axis=1, keepdims=True)
     ids_src[...] = jnp.broadcast_to(wanted, (R, B)).reshape(T, cap, B)
-    put_hot = jnp.where(place_hot, 1.0, 0.0).astype(BF)
+    for copy in copies[3:6]:
+        copy.wait()
 
     peers = V - 1 + T - 1
 
@@ -146,12 +163,10 @@
             return carry
 
         lax.fori_loop(1, T, send, 0)
+        pending.append(lambda: wait_bytes(src.at[pl.ds(0, T - 1)], t_send.at[n]))
 
     def tok_wait(src, buf, n):
         wait_bytes(buf.at[pl.ds(0, T - 1)], t_recv.at[n])
-
-    def tok_done(src, buf, n):
-        wait_bytes(src.at[pl.ds(0, T - 1)], t_send.at[n])
 
     tok_start(ids_src, ids_buf, 0)
 
@@ -181,61 +196,68 @@
             wait_bytes(src, send)
 
     w1_each(w1_go)
+    pending.append(lambda: w1_each(w1_end))
+    pending.append(lambda: w2_done())
 
     arrays = (Wq, Wod)
-    right_hops, left_hops = Y // 2, Y - 1 - Y // 2
-
-    def slab(a, k):
-        return arrays[a].at[pl.ds(Xc * c, Xc), pl.ds(pl.multiple_of(k * B, B), B)]
-
-    def hop(a, h, way):
+    half_up, half_down = Y // 2, Y - 1 - Y // 2
+
+    def block_of(a, i, k):
+        return arrays[a].at[Xc * c + i, pl.ds(pl.multiple_of(k * B, B), B)]
+
+    def hops_of(i, way):
+        return half_up if way == i % 2 else half_down
+
+    def hop(a, i, h, way):
         step = 1 if way == 0 else Y - 1
-        k = (y + (Y - step) * (h - 1)) % Y
-        ref = slab(a, k)
+        ref = block_of(a, i, (y + (Y - step) * (h - 1)) % Y)
         return remote(
-            ref, ref, w2_send.at[a, way, h - 1], w2_recv.at[a, way, h - 1],
+            ref, ref, w2_send.at[a, i, way, h - 1], w2_recv.at[a, i, way, h - 1],
             dev(x, z, (y + step) % Y, c),
         )
 
-    def sibling(a, k, n):
-        ref = slab(a, k)
-        return remote(ref, ref, sib_send.at[a, n], sib_recv.at[a, n], dev(x, z, y, (c + 1) % C))
-
-    def hops_of(way):
-        return right_hops if way == 0 else left_hops
-
-    def arrived(h, way):
-        step = 1 if way == 0 else Y - 1
-        return (y + (Y - step) * h) % Y
+    def sibling(a, i, k, n):
+        ref = block_of(a, i, k)
+        return remote(
+            ref, ref, sib_send.at[a, i, n], sib_recv.at[a, i, n], dev(x, z, y, (c + 1) % C)
+        )
 
     def w2_begin(a):
         wait_bytes(arrays[a].at[pl.ds(0, Xc), pl.ds(0, B)], (w1q_sem, w1o_sem)[a])
+        for i in range(Xc):
+            for way in (0, 1):
+                if hops_of(i, way) >= 1:
+                    hop(a, i, 1, way).start()
+        for i in range(Xc):
+            sibling(a, i, y, 0).start()
+
+    def w2_forward(a, i, h):
+        if i >= Xc:
+            return
         for way in (0, 1):
-            if hops_of(way) >= 1:
-                hop(a, 1, way).start()
-        sibling(a, y, 0).start()
-
-    def sib_slot(h, way):
-        return h if way == 0 else right_hops + h
-
-    def w2_forward(a, h):
+            if h <= hops_of(i, way):
+                hop(a, i, h, way).wait_recv()
+                if h + 1 <= hops_of(i, way):
+                    hop(a, i, h + 1, way).start()
         for way in (0, 1):
-            if h <= hops_of(way):
-                hop(a, h, way).wait_recv()
-                if h + 1 <= hops_of(way):
-                    hop(a, h + 1, way).start()
-                sibling(a, arrived(h, way), sib_slot(h, way)).start()
+            if h <= hops_of(i, way):
+                step = 1 if way == 0 else Y - 1
+                n = h if way == 0 else hops_of(i, 0) + h
+                sibling(a, i, (y + (Y - step) * h) % Y, n).start()
 
     def w2_ready(a):
-        for n in range(Y):
-            wait_bytes(arrays[a].at[pl.ds(0, Xc), pl.ds(0, B)], sib_recv.at[a, n])
-
-    def w2_done(a):
-        for way in (0, 1):
-            for h in range(1, hops_of(way) + 1):
-                hop(a, h, way).wait_send()
-        for n in range(Y):
-            wait_bytes(arrays[a].at[pl.ds(0, Xc), pl.ds(0, B)], sib_send.at[a, n])
+        for i in range(Xc):
+            for n in range(Y):
+                wait_bytes(arrays[a].at[0, pl.ds(0, B)], sib_recv.at[a, i, n])
+
+    def w2_done():
+        for a in (0, 1):
+            for i in range(Xc):
+                for way in (0, 1):
+                    for h in range(1, hops_of(i, way) + 1):
+                        hop(a, i, h, way).wait_send()
+                for n in range(Y):
+                    wait_bytes(arrays[a].at[0, pl.ds(0, B)], sib_send.at[a, i, n])
 
     row = z % X
     at_home = x == row
@@ -252,6 +274,8 @@
         @pl.when(jnp.logical_not(at_home))
         def _():
             remote(src, buf.at[k], e0_send.at[n], e_recv.at[n], dev(row, z, y, c)).start()
+
+        pending.append(lambda: row_done(src, buf, n))
 
     def row_wait(src, buf, n):
         wait_bytes(buf, e_recv.at[n])
@@ -269,6 +293,7 @@
             remote(
                 part.at[to], buf.at[d - 1], rx_send.at[n], rx_recv.at[n], dev(to, z, y, c)
             ).start()
+        pending.append(lambda: wait_bytes(buf, rx_send.at[n]))
 
     def rx_sum(part, buf, n):
         wait_bytes(buf, rx_recv.at[n])
@@ -282,6 +307,7 @@
             remote(
                 buf.at[x], buf.at[x], ax_send.at[n], ax_recv.at[n], dev((x + d) % X, z, y, c)
             ).start()
+        pending.append(lambda: wait_bytes(buf.at[pl.ds(0, X - 1)], ax_send.at[n]))
 
     def ax_wait(buf, n):
         wait_bytes(buf.at[pl.ds(0, X - 1)], ax_recv.at[n])
@@ -311,7 +337,7 @@
             def _():
                 wait_bytes(part.at[k], r_send.at[n, k])
 
-    def spread_back(left, weights, part, buf, n):
+    def spread_back(left, weights, part, buf, n, seen=None):
         step = 2
         for first in range(0, Z, step):
             total = None
@@ -321,6 +347,10 @@
             for k in range(first, first + step):
                 part[k] = total[:, (k - first) * B : (k - first + 1) * B].astype(BF)
                 own_start(part, buf, k, n)
+            if seen is not None:
+                for k in range(first, first + step):
+                    seen(k, part[k].astype(F32))
+        pending.append(lambda: own_done(part, n))
 
     def ar_start(rows, n):
         ar_src[n] = rows
@@ -333,14 +363,17 @@
             return carry
 
         lax.fori_loop(1, V, send, 0)
+        pending.append(lambda: wait_bytes(ar_buf.at[n, pl.ds(1, V - 1)], s_send.at[n]))
 
     def ar_sum(n):
         wait_bytes(ar_buf.at[n, pl.ds(1, V - 1)], s_recv.at[n])
         return rows_to_square(jnp.sum(ar_buf[n], axis=0))
 
-    def ar_done(n):
-        wait_bytes(ar_buf.at[n, pl.ds(1, V - 1)], s_send.at[n])
-
+    for copy in copies[6:]:
+        copy.wait()
+    hw_buf[x] = jnp.broadcast_to(hw_ref[...].astype(F32), (16, B)).astype(BF)
+    ax_start(hw_buf, 3)
+    put_hot = jnp.where(place_hot, 1.0, 0.0).astype(BF)
     place_square = row_to_square(place)
     take_hot = jnp.concatenate(
         [
@@ -349,7 +382,12 @@
         ],
         axis=1,
     ).astype(BF)
-    emb_copy.wait()
+    segment_f = seg_ref[...].astype(F32)
+    same_segment = row_to_square(segment_f) == segment_f
+    labels = row_to_square(lab_ref[...].astype(F32))[:, 0:1]
+    gain = gain_ref[...].astype(F32)
+    head_vector = hw_ref[...].astype(F32)
+    x_src[B : B + 16, :] = jnp.broadcast_to(gain, (16, B)).astype(BF)
     tok_wait(ids_src, ids_buf, 0)
     requested = ids_buf[...].reshape(R, B)
     chunk = 512
@@ -373,13 +411,11 @@
     w2_begin(0)
     for first in range(0, R, B):
         req_out[:, first : first + B] = requested[first : first + B].T[:8]
-    w2_forward(0, 1)
+    w2_forward(0, 0, 1)
+    w2_forward(0, 1, 1)
     tok_wait(row_src, row_buf, 1)
-    inputs = dot(take_hot, row_buf[...].reshape(R, B))
-    features = inputs
-    gain = gain_ref[...].astype(F32)
-    x_src[0:B, :] = inputs.astype(BF)
-    x_src[B : B + 16, :] = jnp.broadcast_to(gain_ref[...].astype(F32), (16, B)).astype(BF)
+    features = dot(take_hot, row_buf[...].reshape(R, B))
+    x_src[0:B, :] = features.astype(BF)
     row_start(x_src, x_buf, 0)
     ar_start(
         columns_to_rows(
@@ -390,30 +426,34 @@
         ),
         0,
     )
-    w2_forward(0, 2)
+    w2_forward(0, 0, 2)
+    w2_forward(0, 1, 2)
     stats = ar_sum(0)
     row_mean = stats[:, 0:1] / D
     variance = stats[:, 1:2] / D - row_mean * row_mean
     inv_std = lax.rsqrt(variance + epsilon)
     centered = (features - row_mean) * inv_std
-    w2_forward(0, 3)
+    w2_forward(0, 0, 3)
+    w2_forward(0, 1, 3)
     row_wait(x_src, x_buf, 0)
     for k in range(Z):
         block = x_buf[k, 0:B, :].astype(F32)
-        block_gain = x_buf[k, B : B + 16, :].astype(F32)[0:1]
-        nrm[:, k * B : (k + 1) * B] = (((block - row_mean) * inv_std) * block_gain).astype(BF)
-    w2_forward(0, 4)
+        block_gain = x_buf[k, B : B + 16, :].astype(F32)[0:8]
+        gains[k] = block_gain
+        normed = ((block - row_mean) * inv_std) * block_gain[0:1]
+        cgain[k] = normed
+        nrm[:, k * B : (k + 1) * B] = normed.astype(BF)
     w2_begin(1)
+    w2_forward(0, 0, 4)
+    w2_forward(0, 1, 4)
     w2_ready(0)
-
     for xx in range(X):
         pq[xx] = dot(nrm[...], Wq[xx]).astype(BF)
     rx_start(pq, pq_buf, 0)
-    w2_forward(1, 1)
+    w2_forward(1, 0, 1)
+    w2_forward(1, 1, 1)
     qkv = rx_sum(pq, pq_buf, 0).astype(BF)
     queries, keys, values = qkv[:, :B], qkv[:, B : 2 * B], qkv[:, 2 * B :]
-    segment_f = seg_ref[...].astype(F32)
-    same_segment = row_to_square(segment_f) == segment_f
     raw = dot_nt(queries, keys) / math.sqrt(B)
     capped = soft_limit * jnp.tanh(raw / soft_limit)
     exps = jnp.where(same_segment, jnp.exp(capped), 0.0)
@@ -421,9 +461,9 @@
     prob_rounded = probabilities.astype(BF)
     h_src[...] = dot(prob_rounded, values).astype(BF)
     row_start(h_src, h_buf, 1)
-    w2_forward(1, 2)
-    w2_forward(1, 3)
-    w2_forward(1, 4)
+    for h in (2, 3, 4):
+        w2_forward(1, 0, h)
+        w2_forward(1, 1, h)
     row_wait(h_src, h_buf, 1)
     w2_ready(1)
 
@@ -441,9 +481,8 @@
         pd[xx] = dot(dense_row, Wod[xx, :, B : 2 * B]).astype(pd.dtype)
     rx_start(pd, pd_buf, 2)
     dense_linear = rx_sum(pd, pd_buf, 2)
-    phi = 0.5 * (1.0 + lax.erf(dense_linear * inv_root_two))
-    activated = dense_linear * phi
-    head_vector = hw_ref[...].astype(F32)
+    dl_buf[x] = dense_linear
+    activated = dense_linear * (0.5 * (1.0 + lax.erf(dense_linear * inv_root_two)))
     ar_start(
         columns_to_rows(
             [
@@ -455,26 +494,30 @@
         ),
         1,
     )
-    gelu_slope = phi + dense_linear * jnp.exp(-0.5 * dense_linear * dense_linear) * inv_root_tau
-    labels = row_to_square(lab_ref[...].astype(F32))[:, 0:1]
+    ax_start(dl_buf, 0)
+    ax_wait(hw_buf, 3)
+    ax_wait(dl_buf, 0)
+    gelus = []
+    for xx in range(X):
+        linear = dl_buf[xx]
+        phi = 0.5 * (1.0 + lax.erf(linear * inv_root_two))
+        slope = phi + linear * jnp.exp(-0.5 * linear * linear) * inv_root_tau
+        gelus.append((linear * phi, slope, hw_buf[xx].astype(F32)[0:1]))
     stats = ar_sum(1)
     head_mean = stats[:, 0:1] / D
     head_scale = lax.rsqrt(stats[:, 1:2] / D - head_mean * head_mean + epsilon)
     weight_sum = stats[:, 3:4]
     logits = head_scale * (stats[:, 2:3] - head_mean * weight_sum)
     logit_grads = loss_scale * (jax.nn.sigmoid(logits) - labels)
-    head_centered = (activated - head_mean) * head_scale
     mean_grads = logit_grads * weight_sum / D
     mean_product = logit_grads * logits / D
-    activated_grads = head_scale * (
-        logit_grads * head_vector - mean_grads - head_centered * mean_product
-    )
-    pre_buf[x] = (activated_grads * gelu_slope).astype(BF)
-    ax_start(pre_buf, 0)
-    ax_wait(pre_buf, 0)
-    spread_back(
-        lambda xx: pre_buf[xx], lambda xx, rows: Wod[xx, rows, B : 2 * B], b1, b1_buf, 0
-    )
+    for xx, (active, slope, vector) in enumerate(gelus):
+        head_centered = (active - head_mean) * head_scale
+        activated_grads = head_scale * (
+            logit_grads * vector - mean_grads - head_centered * mean_product
+        )
+        pre[xx] = (activated_grads * slope).astype(BF)
+    spread_back(lambda xx: pre[xx], lambda xx, rows: Wod[xx, rows, B : 2 * B], b1, b1_buf, 0)
     hidden_grads = own_sum(b1_buf, 0)
     hr_buf[x] = hidden_grads.astype(BF)
     ax_start(hr_buf, 1)
@@ -494,17 +537,15 @@
     g_buf[x] = jnp.concatenate([query_grads, key_grads, value_grads], axis=1).astype(BF)
     ax_start(g_buf, 2)
     ax_wait(g_buf, 2)
-    spread_back(lambda xx: g_buf[xx], lambda xx, rows: Wq[xx, rows, :], b3, b3_buf, 2)
+    sums = [jnp.zeros((B, B), F32), jnp.zeros((B, B), F32)]
+
+    def gather_sums(k, block):
+        sums[0] = sums[0] + block * gains[k, 0:1]
+        sums[1] = sums[1] + block * cgain[k]
+
+    spread_back(lambda xx: g_buf[xx], lambda xx, rows: Wq[xx, rows, :], b3, b3_buf, 2, gather_sums)
+    ar_start(columns_to_rows([jnp.sum(total, axis=1, keepdims=True) for total in sums]), 2)
     scaled = own_sum(b3_buf, 2) * gain
-    ar_start(
-        columns_to_rows(
-            [
-                jnp.sum(scaled, axis=1, keepdims=True),
-                jnp.sum(scaled * centered, axis=1, keepdims=True),
-            ]
-        ),
-        2,
-    )
     stats = ar_sum(2)
     input_grads = hidden_grads + inv_std * (
         scaled - stats[:, 0:1] / D - centered * (stats[:, 1:2] / D)
@@ -515,23 +556,7 @@
     tok_wait(gslot_src, gslot_buf, 2)
     grad_out[...] = gslot_buf[...].reshape(R, B)
 
-    tok_done(ids_src, ids_buf, 0)
-    tok_done(row_src, row_buf, 1)
-    tok_done(gslot_src, gslot_buf, 2)
-    w1_each(w1_end)
-    w2_done(0)
-    w2_done(1)
-    row_done(x_src, x_buf, 0)
-    row_done(h_src, h_buf, 1)
-    row_done(d_src, d_buf, 2)
-    for n, buf in enumerate((pq_buf, po_buf, pd_buf)):
-        wait_bytes(buf, rx_send.at[n])
-    for n, buf in enumerate((pre_buf, hr_buf, g_buf)):
-        wait_bytes(buf.at[pl.ds(0, X - 1)], ax_send.at[n])
-    for n, part in enumerate((b1, b2, b3)):
-        own_done(part, n)
-    for n in range(3):
-        ar_done(n)
+    finish()
 
 
 def table_kernel(tile, grad_ref, req_ref, out_ref):
@@ -562,13 +587,17 @@
             jax.ShapeDtypeStruct((R, B), BF),
             jax.ShapeDtypeStruct((8, R), F32),
         ),
-        in_specs=[pl.BlockSpec(memory_space=pl.ANY)] + [vm] * 10,
+        in_specs=[pl.BlockSpec(memory_space=pltpu.HBM)] * 11,
         out_specs=(vm, vm),
         scratch_shapes=[
             VM((vocab_rows, B), BF),
+            VM((rows, 3 * B), BF),
             VM((rows, 2 * B), BF),
             VM((X, Z * B, 3 * B), BF),
             VM((X, Z * B, 2 * B), BF),
+            VM((1, B), jnp.int32), VM((1, B), jnp.int32), VM((1, B), jnp.int32),
+            VM((1, B), BF), VM((1, B), BF),
+            VM((1, B), jnp.int32), VM((1, B), jnp.int32),
             VM((T, cap, B), F32), VM((T, cap, B), F32),
             VM((T, cap, B), BF), VM((T, cap, B), BF),
             VM((T, cap, B), BF), VM((T, cap, B), BF),
@@ -576,21 +605,23 @@
             VM((B, B), BF), VM((Z, B, B), BF),
             VM((B, B), BF), VM((Z, B, B), BF),
             VM((X, B, 3 * B), BF), VM((X - 1, B, 3 * B), BF),
-            VM((X, B, B), F32), VM((X - 1, B, B), F32),
-            VM((X, B, B), F32), VM((X - 1, B, B), F32),
-            VM((X, B, B), BF), VM((Z, B, B), BF), VM((Z, B, B), BF),
+            VM((X, B, B), BF), VM((X - 1, B, B), BF),
+            VM((X, B, B), BF), VM((X - 1, B, B), BF),
+            VM((Z, B, B), BF), VM((Z, B, B), BF),
             VM((X, B, B), BF), VM((Z, B, B), BF), VM((Z, B, B), BF),
             VM((X, B, 3 * B), BF), VM((Z, B, B), BF), VM((Z, B, B), BF),
-            VM((B, Z * B), BF),
+            VM((B, Z * B), BF), VM((Z, B, B), F32), VM((Z, 8, B), F32),
+            VM((X, B, B), F32), VM((X, B, B), BF), VM((X, 16, B), BF),
             VM((3, 8, B), F32), VM((3, V, 8, B), F32),
-            dma(()), dma(()), dma(()), dma((X // C, 2)),
-            dma((2, 2, right)), dma((2, 2, right)), dma((2, Y)), dma((2, Y)),
+            dma((11,)), dma(()), dma(()), dma((X // C, 2)),
+            dma((2, X // C, 2, right)), dma((2, X // C, 2, right)),
+            dma((2, X // C, Y)), dma((2, X // C, Y)),
             dma((3,)), dma((3,)), dma((3,)), dma((3,)), dma((3,)),
-            dma((3,)), dma((3,)), dma((3,)), dma((3,)),
+            dma((3,)), dma((3,)), dma((4,)), dma((4,)),
             dma((3,)), dma((3, Z)), dma((3,)), dma((3,)),
         ],
         compiler_params=pltpu.CompilerParams(
-            collective_id=0, has_side_effects=True, vmem_limit_bytes=40 * 1024 * 1024
+            collective_id=0, has_side_effects=True, vmem_limit_bytes=60 * 1024 * 1024
         ),
     )(
         embeddings,
@@ -611,6 +642,7 @@
             pl.BlockSpec((8, R), lambda i: (0, 0)),
         ],
         out_specs=pl.BlockSpec((tile, B), lambda i: (i, 0)),
+        compiler_params=pltpu.CompilerParams(vmem_limit_bytes=60 * 1024 * 1024),
     )(grads, requests)
 
 

time: 188 us -> 161 us (0.86)
  Pallas kernels: 178 us -> 160 us
  local copies, waits for them, and re-layouts: 10 us -> 0 us
    pallas_call x1, Pallas kernels: 173 us -> 155 us  [local(): pl.pallas_call(functools.partial(main_kernel, X, Z, Y, C, vocab_rows), ou...]
    unnamed x26 -> x0, local copies, waits for them, and re-layouts: 10 us -> none
where the time goes in v2:
time: 161 us; the launch traced here: 160 us
  Pallas kernels  160 us (99%)
    pallas_call x1, Pallas kernels, local(): pl.pallas_call(functools.partial(main_kernel, X, Z, Y, C, vocab_rows), ou...  155 us
    pallas_call x1, Pallas kernels, local(): pl.pallas_call(functools.partial(table_kernel, tile), grid=(vocab_rows //...  5.21 us

profile of v2, /device:TPU:1, one launch (start us, length us, event | category | flops | bytes accessed | tf_op | source)
XLA Modules:
  0.0 160.4 jit_solution(13420454108756348349)
XLA Ops:
  0.0 155.2 %shard_map.109 = (bf16[256,128]{1,0:T(8,128)(2,1)}, f32[8,256]{1,0:T(8,128)}) custom-call(bf16[8192,128]{1,0:T(8,128)(2,1)} %emb_hbm.1, bf16[1,128]{1,0:T(2,128)(2,1)} %bitcast.4, bf16[256,384]{1,0:T(8,128)(2,1)} %bitcast.3, bf16[256,128]{1,0:T(8,128)(2,1)} %wo_hbm.1, bf16[256,128]{1,0:T(8,128)(2,1)} %wd_hbm.1, bf16[1,128]{1,0:T(2,128)(2,1)} %bitcast.5, ...), custom_call_target="tpu_custom_call" | custom-call | tf_op jit(solution)/shard_map/pallas_call | solution.py:584
  155.2 5.2 %shard_map.110 = bf16[8192,128]{1,0:T(8,128)(2,1)} custom-call(bf16[256,128]{1,0:T(8,128)(2,1)} %get-tuple-element.7.grad_ref, f32[8,256]{1,0:T(8,128)} %get-tuple-element.8.req_ref), custom_call_target="tpu_custom_call" | custom-call | tf_op jit(solution)/shard_map/pallas_call | solution.py:636

commit v3 on v2

--- a/solution.py
+++ b/solution.py
@@ -59,13 +59,13 @@
     grad_out, req_out,
     emb, wq_ref, wod_src, Wq, Wod,
     tok_ref, rep_ref, mask_ref, gain_ref, hw_ref, lab_ref, seg_ref,
-    ids_src, ids_buf, row_src, row_buf, gslot_src, gslot_buf,
+    ids_src, ids_buf, row_src, row_buf, st_src, st_buf, gslot_src, gslot_buf,
     x_src, x_buf, h_src, h_buf, d_src, d_buf,
     pq, pq_buf, po, po_buf, pd, pd_buf,
     b1, b1_buf, hr_buf, b2, b2_buf, g_buf, b3, b3_buf,
     nrm, cgain, gains, dl_buf, pre, hw_buf, ar_src, ar_buf,
     in_sem, w1q_sem, w1o_sem, w1_send, w2_recv, w2_send, sib_recv, sib_send,
-    t_recv, t_send, e_recv, e_send, e0_send, rx_recv, rx_send, ax_recv, ax_send,
+    t_recv, t_send, e_recv, e_send, rx_recv, rx_send, ax_recv, ax_send,
     r_recv, r_send, s_recv, s_send,
 ):
     V, T = X * Z, Y * C
@@ -92,6 +92,7 @@
     def finish():
         for done in pending:
             done()
+        pending.clear()
 
     def wait_bytes(ref, sem):
         pltpu.make_async_copy(ref, ref, sem).wait()
@@ -119,14 +120,22 @@
 
     lax.fori_loop(1, V, greet_vocab, 0)
     lax.fori_loop(1, T, greet_tok, 0)
+    turn = y // (Z // X)
     same_core = (x // Xc) == c
+    from_core = ((x + turn) % X) // Xc
+    other_source = from_core != c
 
     @pl.when(jnp.logical_not(same_core))
     def _():
         for i in range(Xc):
-            pl.semaphore_signal(
-                barrier, inc=1, device_id=dev(Xc * c + i, z, y, x // Xc), device_id_type=MESH
-            )
+            to = dev((Xc * c + i + X - turn) % X, z, y, x // Xc)
+            pl.semaphore_signal(barrier, inc=1, device_id=to, device_id_type=MESH)
+
+    @pl.when(other_source)
+    def _():
+        for i in range(Xc):
+            to = dev(Xc * c + i, z, y, from_core)
+            pl.semaphore_signal(barrier, inc=1, device_id=to, device_id_type=MESH)
 
     for copy in copies[:3]:
         copy.wait()
@@ -144,15 +153,12 @@
     for copy in copies[3:6]:
         copy.wait()
 
-    peers = V - 1 + T - 1
-
-    @pl.when(same_core)
-    def _():
-        pl.semaphore_wait(barrier, peers)
-
-    @pl.when(jnp.logical_not(same_core))
-    def _():
-        pl.semaphore_wait(barrier, peers + Xc)
+    pl.semaphore_wait(
+        barrier,
+        V - 1 + T - 1
+        + Xc * jnp.where(same_core, 0, 1)
+        + Xc * jnp.where(other_source, 1, 0),
+    )
 
     def tok_start(src, buf, n):
         buf[t] = src[t]
@@ -172,7 +178,7 @@
 
     def w1_each(act):
         for i in range(Xc):
-            xd, cd = Xc * c + i, x // Xc
+            xd, cd = (Xc * c + i + X - turn) % X, x // Xc
             mine = (xd == x) & same_core
             rows = pl.ds(i * B, B)
             dst_rows = pl.ds(pl.multiple_of(y * B, B), B)
@@ -212,14 +218,14 @@
         step = 1 if way == 0 else Y - 1
         ref = block_of(a, i, (y + (Y - step) * (h - 1)) % Y)
         return remote(
-            ref, ref, w2_send.at[a, i, way, h - 1], w2_recv.at[a, i, way, h - 1],
+            ref, ref, w2_send.at[a, i], w2_recv.at[a, i, way, h - 1],
             dev(x, z, (y + step) % Y, c),
         )
 
-    def sibling(a, i, k, n):
+    def sibling(a, i, k):
         ref = block_of(a, i, k)
         return remote(
-            ref, ref, sib_send.at[a, i, n], sib_recv.at[a, i, n], dev(x, z, y, (c + 1) % C)
+            ref, ref, sib_send.at[a, i], sib_recv.at[a, i], dev(x, z, y, (c + 1) % C)
         )
 
     def w2_begin(a):
@@ -229,7 +235,7 @@
                 if hops_of(i, way) >= 1:
                     hop(a, i, 1, way).start()
         for i in range(Xc):
-            sibling(a, i, y, 0).start()
+            sibling(a, i, y).start()
 
     def w2_forward(a, i, h):
         if i >= Xc:
@@ -242,50 +248,48 @@
         for way in (0, 1):
             if h <= hops_of(i, way):
                 step = 1 if way == 0 else Y - 1
-                n = h if way == 0 else hops_of(i, 0) + h
-                sibling(a, i, (y + (Y - step) * h) % Y, n).start()
+                sibling(a, i, (y + (Y - step) * h) % Y).start()
 
     def w2_ready(a):
         for i in range(Xc):
-            for n in range(Y):
-                wait_bytes(arrays[a].at[0, pl.ds(0, B)], sib_recv.at[a, i, n])
+            wait_bytes(arrays[a].at[0], sib_recv.at[a, i])
 
     def w2_done():
         for a in (0, 1):
             for i in range(Xc):
-                for way in (0, 1):
-                    for h in range(1, hops_of(i, way) + 1):
-                        hop(a, i, h, way).wait_send()
-                for n in range(Y):
-                    wait_bytes(arrays[a].at[0, pl.ds(0, B)], sib_send.at[a, i, n])
-
-    row = z % X
+                wait_bytes(arrays[a].at[0, pl.ds(0, (Y - 1) * B)], w2_send.at[a, i])
+                wait_bytes(arrays[a].at[0], sib_send.at[a, i])
+
+    row = (z + X - x) % X
     at_home = x == row
+
+    def block_done(ref, sem):
+        @pl.when(at_home)
+        def _():
+            wait_bytes(ref.at[pl.ds(0, Z - 1)], sem)
+
+        @pl.when(jnp.logical_not(at_home))
+        def _():
+            wait_bytes(ref, sem)
 
     def row_start(src, buf, n):
         k = v // X
-        for j in list(range(1, Z)):
-            remote(src, buf.at[k], e_send.at[n], e_recv.at[n], dev(row, (z + j) % Z, y, c)).start()
-
-        @pl.when(at_home)
-        def _():
-            pltpu.make_async_copy(src, buf.at[k], e_recv.at[n]).start()
-
-        @pl.when(jnp.logical_not(at_home))
-        def _():
-            remote(src, buf.at[k], e0_send.at[n], e_recv.at[n], dev(row, z, y, c)).start()
-
-        pending.append(lambda: row_done(src, buf, n))
+        for j in range(Z):
+            zd = (z + x + j) % Z
+            mine = at_home & (zd == z)
+
+            @pl.when(mine)
+            def _():
+                pltpu.make_async_copy(src, buf.at[k], e_recv.at[n]).start()
+
+            @pl.when(jnp.logical_not(mine))
+            def _():
+                remote(src, buf.at[k], e_send.at[n], e_recv.at[n], dev(row, zd, y, c)).start()
+
+        pending.append(lambda: block_done(buf, e_send.at[n]))
 
     def row_wait(src, buf, n):
         wait_bytes(buf, e_recv.at[n])
-
-    def row_done(src, buf, n):
-        wait_bytes(buf.at[pl.ds(0, Z - 1)], e_send.at[n])
-
-        @pl.when(jnp.logical_not(at_home))
-        def _():
-            wait_bytes(src, e0_send.at[n])
 
     def rx_start(part, buf, n):
         for d in range(1, X):
@@ -312,17 +316,21 @@
     def ax_wait(buf, n):
         wait_bytes(buf.at[pl.ds(0, X - 1)], ax_recv.at[n])
 
-    def own_start(part, buf, k, n):
-        to = X * k + x
-        mine = to == v
-
-        @pl.when(mine)
-        def _():
-            pltpu.make_async_copy(part.at[k], buf.at[z], r_recv.at[n]).start()
-
-        @pl.when(jnp.logical_not(mine))
-        def _():
-            remote(part.at[k], buf.at[z], r_send.at[n, k], r_recv.at[n], (to, t)).start()
+    def own_start(part, buf, n):
+        for j in range(Z):
+            k = (z + j) % Z
+            to = X * k + (x + k // (Z // X)) % X
+            mine = to == v
+
+            @pl.when(mine)
+            def _():
+                pltpu.make_async_copy(part.at[k], buf.at[z], r_recv.at[n]).start()
+
+            @pl.when(jnp.logical_not(mine))
+            def _():
+                remote(part.at[k], buf.at[z], r_send.at[n], r_recv.at[n], (to, t)).start()
+
+        pending.append(lambda: block_done(part, r_send.at[n]))
 
     def own_sum(buf, n):
         wait_bytes(buf, r_recv.at[n])
@@ -330,12 +338,6 @@
         for k in range(1, Z):
             total = total + buf[k].astype(F32)
         return total
-
-    def own_done(part, n):
-        for k in range(Z):
-            @pl.when(X * k + x != v)
-            def _():
-                wait_bytes(part.at[k], r_send.at[n, k])
 
     def spread_back(left, weights, part, buf, n, seen=None):
         step = 2
@@ -346,11 +348,9 @@
                 total = term if total is None else total + term
             for k in range(first, first + step):
                 part[k] = total[:, (k - first) * B : (k - first + 1) * B].astype(BF)
-                own_start(part, buf, k, n)
-            if seen is not None:
-                for k in range(first, first + step):
-                    seen(k, part[k].astype(F32))
-        pending.append(lambda: own_done(part, n))
+        if seen is not None:
+            seen()
+        own_start(part, buf, n)
 
     def ar_start(rows, n):
         ar_src[n] = rows
@@ -392,6 +392,8 @@
     requested = ids_buf[...].reshape(R, B)
     chunk = 512
 
+    w2_begin(0)
+
     def fetch(i, total):
         base = i * chunk
         hot = jnp.concatenate(
@@ -408,7 +410,12 @@
     fetched = lax.fori_loop(0, vocab_rows // chunk, fetch, jnp.zeros((R, B), F32))
     row_src[...] = fetched.astype(BF).reshape(T, cap, B)
     tok_start(row_src, row_buf, 1)
-    w2_begin(0)
+    row_sums = []
+    for first in range(0, R, B):
+        piece = fetched[first : first + B]
+        row_sums.append(jnp.sum(piece, axis=1, keepdims=True))
+        row_sums.append(jnp.sum(piece * piece, axis=1, keepdims=True))
+    ar_start(columns_to_rows(row_sums), 0)
     for first in range(0, R, B):
         req_out[:, first : first + B] = requested[first : first + B].T[:8]
     w2_forward(0, 0, 1)
@@ -417,24 +424,29 @@
     features = dot(take_hot, row_buf[...].reshape(R, B))
     x_src[0:B, :] = features.astype(BF)
     row_start(x_src, x_buf, 0)
-    ar_start(
-        columns_to_rows(
-            [
-                jnp.sum(features, axis=1, keepdims=True),
-                jnp.sum(features * features, axis=1, keepdims=True),
-            ]
-        ),
-        0,
-    )
+    stats = ar_sum(0)
+    lane = iota((B, B), 1)
+    for first in range(0, R, B):
+        i = 2 * (first // B)
+        pair = jnp.where(lane == 0, stats[:, i : i + 1], stats[:, i + 1 : i + 2])
+        st_src[first // cap : (first + B) // cap] = pair.reshape(B // cap, cap, B)
+    tok_start(st_src, st_buf, 3)
     w2_forward(0, 0, 2)
     w2_forward(0, 1, 2)
-    stats = ar_sum(0)
+    tok_wait(st_src, st_buf, 3)
+    stats = jnp.dot(
+        take_hot.astype(F32),
+        st_buf[...].reshape(R, B),
+        preferred_element_type=F32,
+        precision=lax.Precision.HIGHEST,
+    )
     row_mean = stats[:, 0:1] / D
     variance = stats[:, 1:2] / D - row_mean * row_mean
     inv_std = lax.rsqrt(variance + epsilon)
     centered = (features - row_mean) * inv_std
     w2_forward(0, 0, 3)
     w2_forward(0, 1, 3)
+    w2_begin(1)
     row_wait(x_src, x_buf, 0)
     for k in range(Z):
         block = x_buf[k, 0:B, :].astype(F32)
@@ -443,7 +455,6 @@
         normed = ((block - row_mean) * inv_std) * block_gain[0:1]
         cgain[k] = normed
         nrm[:, k * B : (k + 1) * B] = normed.astype(BF)
-    w2_begin(1)
     w2_forward(0, 0, 4)
     w2_forward(0, 1, 4)
     w2_ready(0)
@@ -537,14 +548,24 @@
     g_buf[x] = jnp.concatenate([query_grads, key_grads, value_grads], axis=1).astype(BF)
     ax_start(g_buf, 2)
     ax_wait(g_buf, 2)
-    sums = [jnp.zeros((B, B), F32), jnp.zeros((B, B), F32)]
-
-    def gather_sums(k, block):
-        sums[0] = sums[0] + block * gains[k, 0:1]
-        sums[1] = sums[1] + block * cgain[k]
-
-    spread_back(lambda xx: g_buf[xx], lambda xx, rows: Wq[xx, rows, :], b3, b3_buf, 2, gather_sums)
-    ar_start(columns_to_rows([jnp.sum(total, axis=1, keepdims=True) for total in sums]), 2)
+    def send_sums():
+        plain, weighted = jnp.zeros((B, B), F32), jnp.zeros((B, B), F32)
+        for k in range(Z):
+            block = b3[k].astype(F32)
+            plain = plain + block * gains[k, 0:1]
+            weighted = weighted + block * cgain[k]
+        columns = [jnp.sum(total, axis=1, keepdims=True) for total in (plain, weighted)]
+        ar_start(columns_to_rows(columns), 2)
+
+    old = list(pending)
+    pending.clear()
+
+    def finish_old():
+        for done in old:
+            done()
+
+    spread_back(lambda xx: g_buf[xx], lambda xx, rows: Wq[xx, rows, :], b3, b3_buf, 2, send_sums)
+    finish_old()
     scaled = own_sum(b3_buf, 2) * gain
     stats = ar_sum(2)
     input_grads = hidden_grads + inv_std * (
@@ -560,11 +581,15 @@
 
 
 def table_kernel(tile, grad_ref, req_ref, out_ref):
-    base = pl.program_id(0) * tile
-    hot = jnp.where(
-        (iota((tile, req_ref.shape[1]), 0) + base).astype(F32) == req_ref[0:1, :], 1.0, 0.0
-    ).astype(BF)
-    out_ref[...] = dot(hot, grad_ref[...]).astype(BF)
+    wanted = req_ref[0:1, :]
+    group = jnp.floor(wanted * (1.0 / B))
+    within = jnp.where(iota((B, wanted.shape[1]), 0).astype(F32) == wanted - group * B, 1.0, 0.0)
+    within = within.astype(BF)
+    grads = grad_ref[...]
+    first = pl.program_id(0) * (tile // B)
+    for g in range(tile // B):
+        here = jnp.where(group == (first + g).astype(F32), 1.0, 0.0).astype(BF)
+        out_ref[g * B : (g + 1) * B, :] = dot(within * here, grads).astype(BF)
 
 
 def local(
@@ -600,6 +625,7 @@
             VM((1, B), jnp.int32), VM((1, B), jnp.int32),
             VM((T, cap, B), F32), VM((T, cap, B), F32),
             VM((T, cap, B), BF), VM((T, cap, B), BF),
+            VM((T, cap, B), F32), VM((T, cap, B), F32),
             VM((T, cap, B), BF), VM((T, cap, B), BF),
             VM((B + 16, B), BF), VM((Z, B + 16, B), BF),
             VM((B, B), BF), VM((Z, B, B), BF),
@@ -614,11 +640,11 @@
             VM((X, B, B), F32), VM((X, B, B), BF), VM((X, 16, B), BF),
             VM((3, 8, B), F32), VM((3, V, 8, B), F32),
             dma((11,)), dma(()), dma(()), dma((X // C, 2)),
-            dma((2, X // C, 2, right)), dma((2, X // C, 2, right)),
-            dma((2, X // C, Y)), dma((2, X // C, Y)),
-            dma((3,)), dma((3,)), dma((3,)), dma((3,)), dma((3,)),
+            dma((2, X // C, 2, right)), dma((2, X // C)),
+            dma((2, X // C)), dma((2, X // C)),
+            dma((4,)), dma((4,)), dma((3,)), dma((3,)),
             dma((3,)), dma((3,)), dma((4,)), dma((4,)),
-            dma((3,)), dma((3, Z)), dma((3,)), dma((3,)),
+            dma((3,)), dma((3,)), dma((3,)), dma((3,)),
         ],
         compiler_params=pltpu.CompilerParams(
             collective_id=0, has_side_effects=True, vmem_limit_bytes=60 * 1024 * 1024

time: 161 us -> 143 us (0.89)
  Pallas kernels: 160 us -> 143 us
    pallas_call x1, Pallas kernels: 155 us -> 138 us  [local(): pl.pallas_call(functools.partial(main_kernel, X, Z, Y, C, vocab_rows), ou...]
where the time goes in v3:
time: 143 us
  Pallas kernels  143 us (100%)
    pallas_call x1, Pallas kernels, local(): pl.pallas_call(functools.partial(main_kernel, X, Z, Y, C, vocab_rows), ou...  138 us
    pallas_call x1, Pallas kernels, local(): pl.pallas_call(functools.partial(table_kernel, tile), grid=(vocab_rows //...  5.11 us

profile of v3, /device:TPU:1, one launch (start us, length us, event | category | flops | bytes accessed | tf_op | source)
XLA Modules:
  0.0 143.1 jit_solution(10812325768268448792)
XLA Ops:
  0.0 137.9 %shard_map.109 = (bf16[256,128]{1,0:T(8,128)(2,1)}, f32[8,256]{1,0:T(8,128)}) custom-call(bf16[8192,128]{1,0:T(8,128)(2,1)} %emb_hbm.1, bf16[1,128]{1,0:T(2,128)(2,1)} %bitcast.4, bf16[256,384]{1,0:T(8,128)(2,1)} %bitcast.3, bf16[256,128]{1,0:T(8,128)(2,1)} %wo_hbm.1, bf16[256,128]{1,0:T(8,128)(2,1)} %wd_hbm.1, bf16[1,128]{1,0:T(2,128)(2,1)} %bitcast.5, ...), custom_call_target="tpu_custom_call" | custom-call | tf_op jit(solution)/shard_map/pallas_call | solution.py:609
  137.9 5.1 %shard_map.110 = bf16[8192,128]{1,0:T(8,128)(2,1)} custom-call(bf16[256,128]{1,0:T(8,128)(2,1)} %get-tuple-element.7.grad_ref, f32[8,256]{1,0:T(8,128)} %get-tuple-element.8.req_ref), custom_call_target="tpu_custom_call" | custom-call | tf_op jit(solution)/shard_map/pallas_call | solution.py:662

commit v4 on v3

--- a/solution.py
+++ b/solution.py
@@ -81,6 +81,9 @@
     def dev(xx, zz, yy, cc):
         return (xx * Z + zz, yy * C + cc)
 
+    def far_first(i, size):
+        return size // 2 + ((i + 1) // 2) * (1 - 2 * (i % 2))
+
     def remote(src, dst, send, recv, device):
         return pltpu.make_async_remote_copy(
             src_ref=src, dst_ref=dst, send_sem=send, recv_sem=recv,
@@ -150,8 +153,6 @@
     place_hot = iota((R, B), 0).astype(F32) == place
     wanted = jnp.sum(jnp.where(place_hot, offset, 0.0), axis=1, keepdims=True)
     ids_src[...] = jnp.broadcast_to(wanted, (R, B)).reshape(T, cap, B)
-    for copy in copies[3:6]:
-        copy.wait()
 
     pl.semaphore_wait(
         barrier,
@@ -163,12 +164,13 @@
     def tok_start(src, buf, n):
         buf[t] = src[t]
 
-        def send(d, carry):
-            to = (t + d) % T
+        def send(i, carry):
+            cd = (c + C - 1 - i % C) % C
+            to = (y + far_first(i // C, Y)) % Y * C + cd
             remote(src.at[to], buf.at[t], t_send.at[n], t_recv.at[n], (v, to)).start()
             return carry
 
-        lax.fori_loop(1, T, send, 0)
+        lax.fori_loop(0, T - 1, send, 0)
         pending.append(lambda: wait_bytes(src.at[pl.ds(0, T - 1)], t_send.at[n]))
 
     def tok_wait(src, buf, n):
@@ -201,6 +203,8 @@
         def _():
             wait_bytes(src, send)
 
+    for copy in copies[3:6]:
+        copy.wait()
     w1_each(w1_go)
     pending.append(lambda: w1_each(w1_end))
     pending.append(lambda: w2_done())
@@ -275,7 +279,7 @@
     def row_start(src, buf, n):
         k = v // X
         for j in range(Z):
-            zd = (z + x + j) % Z
+            zd = (z + far_first(j, Z)) % Z
             mine = at_home & (zd == z)
 
             @pl.when(mine)
@@ -292,7 +296,7 @@
         wait_bytes(buf, e_recv.at[n])
 
     def rx_start(part, buf, n):
-        for d in range(1, X):
+        for d in [far_first(i, X) for i in range(X - 1)]:
             to = (x + d) % X
             remote(
                 part.at[to], buf.at[d - 1], rx_send.at[n], rx_recv.at[n], dev(to, z, y, c)
@@ -307,7 +311,7 @@
         return total
 
     def ax_start(buf, n):
-        for d in range(1, X):
+        for d in [far_first(i, X) for i in range(X - 1)]:
             remote(
                 buf.at[x], buf.at[x], ax_send.at[n], ax_recv.at[n], dev((x + d) % X, z, y, c)
             ).start()
@@ -318,9 +322,10 @@
 
     def own_start(part, buf, n):
         for j in range(Z):
-            k = (z + j) % Z
-            to = X * k + (x + k // (Z // X)) % X
-            mine = to == v
+            zd = (z + far_first(j, Z)) % Z
+            xd = (zd % X + X - x) % X
+            k = xd * (Z // X) + zd // X
+            mine = (xd == x) & (zd == z)
 
             @pl.when(mine)
             def _():
@@ -328,7 +333,8 @@
 
             @pl.when(jnp.logical_not(mine))
             def _():
-                remote(part.at[k], buf.at[z], r_send.at[n], r_recv.at[n], (to, t)).start()
+                to = dev(xd, zd, y, c)
+                remote(part.at[k], buf.at[z], r_send.at[n], r_recv.at[n], to).start()
 
         pending.append(lambda: block_done(part, r_send.at[n]))
 
@@ -356,13 +362,12 @@
         ar_src[n] = rows
         ar_buf[n, 0] = rows
 
-        def send(d, carry):
-            remote(
-                ar_src.at[n], ar_buf.at[n, d], s_send.at[n], s_recv.at[n], ((v + d) % V, t)
-            ).start()
+        def send(i, carry):
+            to = dev((x + far_first(i % X, X)) % X, (z + far_first(i // X, Z)) % Z, y, c)
+            remote(ar_src.at[n], ar_buf.at[n, i + 1], s_send.at[n], s_recv.at[n], to).start()
             return carry
 
-        lax.fori_loop(1, V, send, 0)
+        lax.fori_loop(0, V - 1, send, 0)
         pending.append(lambda: wait_bytes(ar_buf.at[n, pl.ds(1, V - 1)], s_send.at[n]))
 
     def ar_sum(n):
@@ -425,14 +430,17 @@
     x_src[0:B, :] = features.astype(BF)
     row_start(x_src, x_buf, 0)
     stats = ar_sum(0)
+    w2_forward(0, 0, 2)
     lane = iota((B, B), 1)
     for first in range(0, R, B):
         i = 2 * (first // B)
         pair = jnp.where(lane == 0, stats[:, i : i + 1], stats[:, i + 1 : i + 2])
         st_src[first // cap : (first + B) // cap] = pair.reshape(B // cap, cap, B)
     tok_start(st_src, st_buf, 3)
-    w2_forward(0, 0, 2)
     w2_forward(0, 1, 2)
+    w2_forward(0, 0, 3)
+    w2_forward(0, 1, 3)
+    w2_begin(1)
     tok_wait(st_src, st_buf, 3)
     stats = jnp.dot(
         take_hot.astype(F32),
@@ -444,9 +452,6 @@
     variance = stats[:, 1:2] / D - row_mean * row_mean
     inv_std = lax.rsqrt(variance + epsilon)
     centered = (features - row_mean) * inv_std
-    w2_forward(0, 0, 3)
-    w2_forward(0, 1, 3)
-    w2_begin(1)
     row_wait(x_src, x_buf, 0)
     for k in range(Z):
         block = x_buf[k, 0:B, :].astype(F32)
@@ -457,12 +462,14 @@
         nrm[:, k * B : (k + 1) * B] = normed.astype(BF)
     w2_forward(0, 0, 4)
     w2_forward(0, 1, 4)
+    w2_forward(1, 0, 1)
+    w2_forward(1, 1, 1)
     w2_ready(0)
     for xx in range(X):
         pq[xx] = dot(nrm[...], Wq[xx]).astype(BF)
     rx_start(pq, pq_buf, 0)
-    w2_forward(1, 0, 1)
-    w2_forward(1, 1, 1)
+    w2_forward(1, 0, 2)
+    w2_forward(1, 1, 2)
     qkv = rx_sum(pq, pq_buf, 0).astype(BF)
     queries, keys, values = qkv[:, :B], qkv[:, B : 2 * B], qkv[:, 2 * B :]
     raw = dot_nt(queries, keys) / math.sqrt(B)
@@ -472,7 +479,7 @@
     prob_rounded = probabilities.astype(BF)
     h_src[...] = dot(prob_rounded, values).astype(BF)
     row_start(h_src, h_buf, 1)
-    for h in (2, 3, 4):
+    for h in (3, 4):
         w2_forward(1, 0, h)
         w2_forward(1, 1, h)
     row_wait(h_src, h_buf, 1)
@@ -658,7 +665,7 @@
         head_weight.reshape(1, B),
         token_ids, replace_ids, masked, labels, segments,
     )
-    tile = min(1024, vocab_rows)
+    tile = min(4096, vocab_rows)
     return pl.pallas_call(
         functools.partial(table_kernel, tile),
         grid=(vocab_rows // tile,),

time: 143 us -> 134 us (0.937)
  Pallas kernels: 143 us -> 133 us
    pallas_call x1, Pallas kernels: 138 us -> 130 us  [local(): pl.pallas_call(functools.partial(main_kernel, X, Z, Y, C, vocab_rows), ou...]
    pallas_call x1, Pallas kernels: 5.11 us -> 3.24 us  [local(): pl.pallas_call(functools.partial(table_kernel, tile), grid=(vocab_rows //...]
where the time goes in v4:
time: 134 us; the launch traced here: 133 us
  Pallas kernels  133 us (99%)
    pallas_call x1, Pallas kernels, local(): pl.pallas_call(functools.partial(main_kernel, X, Z, Y, C, vocab_rows), ou...  130 us
    pallas_call x1, Pallas kernels, local(): pl.pallas_call(functools.partial(table_kernel, tile), grid=(vocab_rows //...  3.24 us

profile of v4, /device:TPU:1, one launch (start us, length us, event | category | flops | bytes accessed | tf_op | source)
XLA Modules:
  0.0 133.5 jit_solution(10187423305025130599)
XLA Ops:
  0.0 130.2 %shard_map.109 = (bf16[256,128]{1,0:T(8,128)(2,1)}, f32[8,256]{1,0:T(8,128)}) custom-call(bf16[8192,128]{1,0:T(8,128)(2,1)} %emb_hbm.1, bf16[1,128]{1,0:T(2,128)(2,1)} %bitcast.4, bf16[256,384]{1,0:T(8,128)(2,1)} %bitcast.3, bf16[256,128]{1,0:T(8,128)(2,1)} %wo_hbm.1, bf16[256,128]{1,0:T(8,128)(2,1)} %wd_hbm.1, bf16[1,128]{1,0:T(2,128)(2,1)} %bitcast.5, ...), custom_call_target="tpu_custom_call" | custom-call | tf_op jit(solution)/shard_map/pallas_call | solution.py:616
  130.2 3.2 %shard_map.110 = bf16[8192,128]{1,0:T(8,128)(2,1)} custom-call(bf16[256,128]{1,0:T(8,128)(2,1)} %get-tuple-element.7.grad_ref, f32[8,256]{1,0:T(8,128)} %get-tuple-element.8.req_ref), custom_call_target="tpu_custom_call" | custom-call | tf_op jit(solution)/shard_map/pallas_call | solution.py:669

commit v5 on v4

--- a/solution.py
+++ b/solution.py
@@ -60,7 +60,7 @@
     emb, wq_ref, wod_src, Wq, Wod,
     tok_ref, rep_ref, mask_ref, gain_ref, hw_ref, lab_ref, seg_ref,
     ids_src, ids_buf, row_src, row_buf, st_src, st_buf, gslot_src, gslot_buf,
-    x_src, x_buf, h_src, h_buf, d_src, d_buf,
+    g_src, g_all, x_src, x_buf, h_src, h_buf, d_src, d_buf,
     pq, pq_buf, po, po_buf, pd, pd_buf,
     b1, b1_buf, hr_buf, b2, b2_buf, g_buf, b3, b3_buf,
     nrm, cgain, gains, dl_buf, pre, hw_buf, ar_src, ar_buf,
@@ -100,6 +100,14 @@
     def wait_bytes(ref, sem):
         pltpu.make_async_copy(ref, ref, sem).wait()
 
+    def step_of(way):
+        return 1 if way == 0 else Y - 1
+
+    half_up, half_down = Y // 2, Y - 1 - Y // 2
+
+    def hops_of(i, way):
+        return half_up if way == i % 2 else half_down
+
     wanted_here = (
         (tok_hbm, tok_ref), (rep_hbm, rep_ref), (mask_hbm, mask_ref),
         (wq_hbm, wq_ref), (wo_hbm, wod_src.at[:, pl.ds(0, B)]),
@@ -139,6 +147,17 @@
         for i in range(Xc):
             to = dev(Xc * c + i, z, y, from_core)
             pl.semaphore_signal(barrier, inc=1, device_id=to, device_id_type=MESH)
+
+    ways = [way for way in (0, 1) if hops_of(0, way) >= 1]
+    for way in ways:
+        ahead, behind = (y + step_of(way)) % Y, (y + Y - step_of(way)) % Y
+        sender = ((x + behind // (Z // X)) % X) // Xc
+        for i in range(Xc):
+            for to in (
+                dev((Xc * c + i + X - turn) % X, z, ahead, x // Xc),
+                dev(Xc * c + i, z, behind, sender),
+            ):
+                pl.semaphore_signal(barrier, inc=1, device_id=to, device_id_type=MESH)
 
     for copy in copies[:3]:
         copy.wait()
@@ -156,7 +175,7 @@
 
     pl.semaphore_wait(
         barrier,
-        V - 1 + T - 1
+        V - 1 + T - 1 + 2 * Xc * len(ways)
         + Xc * jnp.where(same_core, 0, 1)
         + Xc * jnp.where(other_source, 1, 0),
     )
@@ -179,17 +198,23 @@
     tok_start(ids_src, ids_buf, 0)
 
     def w1_each(act):
-        for i in range(Xc):
-            xd, cd = (Xc * c + i + X - turn) % X, x // Xc
-            mine = (xd == x) & same_core
-            rows = pl.ds(i * B, B)
-            dst_rows = pl.ds(pl.multiple_of(y * B, B), B)
-            q = (wq_ref.at[rows], Wq.at[x, dst_rows], w1q_sem)
-            o = (wod_src.at[rows], Wod.at[x, dst_rows], w1o_sem)
-            for a, (src, dst, sem) in enumerate((q, o)):
-                act(mine, src, dst, sem, w1_send.at[i, a], dev(xd, z, y, cd))
+        first, cd = pl.multiple_of(y * B, B), x // Xc
+        for a, (src, dst) in enumerate(((wq_ref, Wq), (wod_src, Wod))):
+            for i in range(Xc):
+                xd = (Xc * c + i + X - turn) % X
+                mine = (xd == x) & same_core
+                piece, place_ = src.at[pl.ds(i * B, B)], dst.at[x, pl.ds(first, B)]
+                for way in ways if a == 0 else ():
+                    to = dev(xd, z, (y + step_of(way)) % Y, cd)
+                    act(None, piece, place_, w1q_sem.at[1 + way], w1_send.at[i, 2 + way], to)
+                sem = w1q_sem.at[0] if a == 0 else w1o_sem
+                act(mine, piece, place_, sem, w1_send.at[i, a], dev(xd, z, y, cd))
 
     def w1_go(mine, src, dst, sem, send, device):
+        if mine is None:
+            remote(src, dst, send, sem, device).start()
+            return
+
         @pl.when(mine)
         def _():
             pltpu.make_async_copy(src, dst, sem).start()
@@ -199,6 +224,10 @@
             remote(src, dst, send, sem, device).start()
 
     def w1_end(mine, src, dst, sem, send, device):
+        if mine is None:
+            wait_bytes(src, send)
+            return
+
         @pl.when(jnp.logical_not(mine))
         def _():
             wait_bytes(src, send)
@@ -210,13 +239,8 @@
     pending.append(lambda: w2_done())
 
     arrays = (Wq, Wod)
-    half_up, half_down = Y // 2, Y - 1 - Y // 2
-
     def block_of(a, i, k):
         return arrays[a].at[Xc * c + i, pl.ds(pl.multiple_of(k * B, B), B)]
-
-    def hops_of(i, way):
-        return half_up if way == i % 2 else half_down
 
     def hop(a, i, h, way):
         step = 1 if way == 0 else Y - 1
@@ -232,8 +256,21 @@
             ref, ref, sib_send.at[a, i], sib_recv.at[a, i], dev(x, z, y, (c + 1) % C)
         )
 
+    def w2_first():
+        whole = Wq.at[pl.ds(0, Xc), pl.ds(0, B)]
+        for way in ways:
+            wait_bytes(whole, w1q_sem.at[1 + way])
+            for i in range(Xc):
+                if hops_of(i, way) >= 2:
+                    hop(0, i, 2, way).start()
+        wait_bytes(whole, w1q_sem.at[0])
+        for i in range(Xc):
+            sibling(0, i, y).start()
+            for way in ways:
+                sibling(0, i, (y + Y - step_of(way)) % Y).start()
+
     def w2_begin(a):
-        wait_bytes(arrays[a].at[pl.ds(0, Xc), pl.ds(0, B)], (w1q_sem, w1o_sem)[a])
+        wait_bytes(Wod.at[pl.ds(0, Xc), pl.ds(0, B)], w1o_sem)
         for i in range(Xc):
             for way in (0, 1):
                 if hops_of(i, way) >= 1:
@@ -261,7 +298,9 @@
     def w2_done():
         for a in (0, 1):
             for i in range(Xc):
-                wait_bytes(arrays[a].at[0, pl.ds(0, (Y - 1) * B)], w2_send.at[a, i])
+                sent = Y - 1 - (len(ways) if a == 0 else 0)
+                if sent:
+                    wait_bytes(arrays[a].at[0, pl.ds(0, sent * B)], w2_send.at[a, i])
                 wait_bytes(arrays[a].at[0], sib_send.at[a, i])
 
     row = (z + X - x) % X
@@ -392,12 +431,12 @@
     labels = row_to_square(lab_ref[...].astype(F32))[:, 0:1]
     gain = gain_ref[...].astype(F32)
     head_vector = hw_ref[...].astype(F32)
-    x_src[B : B + 16, :] = jnp.broadcast_to(gain, (16, B)).astype(BF)
+    g_src[...] = jnp.broadcast_to(gain, (16, B)).astype(BF)
+    row_start(g_src, g_all, 3)
     tok_wait(ids_src, ids_buf, 0)
     requested = ids_buf[...].reshape(R, B)
     chunk = 512
 
-    w2_begin(0)
 
     def fetch(i, total):
         base = i * chunk
@@ -421,23 +460,22 @@
         row_sums.append(jnp.sum(piece, axis=1, keepdims=True))
         row_sums.append(jnp.sum(piece * piece, axis=1, keepdims=True))
     ar_start(columns_to_rows(row_sums), 0)
-    for first in range(0, R, B):
-        req_out[:, first : first + B] = requested[first : first + B].T[:8]
-    w2_forward(0, 0, 1)
-    w2_forward(0, 1, 1)
+    w2_first()
     tok_wait(row_src, row_buf, 1)
     features = dot(take_hot, row_buf[...].reshape(R, B))
-    x_src[0:B, :] = features.astype(BF)
+    x_src[...] = features.astype(BF)
     row_start(x_src, x_buf, 0)
+    w2_forward(0, 0, 2)
+    w2_forward(0, 1, 2)
     stats = ar_sum(0)
-    w2_forward(0, 0, 2)
     lane = iota((B, B), 1)
     for first in range(0, R, B):
         i = 2 * (first // B)
         pair = jnp.where(lane == 0, stats[:, i : i + 1], stats[:, i + 1 : i + 2])
         st_src[first // cap : (first + B) // cap] = pair.reshape(B // cap, cap, B)
     tok_start(st_src, st_buf, 3)
-    w2_forward(0, 1, 2)
+    for first in range(0, R, B):
+        req_out[:, first : first + B] = requested[first : first + B].T[:8]
     w2_forward(0, 0, 3)
     w2_forward(0, 1, 3)
     w2_begin(1)
@@ -452,10 +490,11 @@
     variance = stats[:, 1:2] / D - row_mean * row_mean
     inv_std = lax.rsqrt(variance + epsilon)
     centered = (features - row_mean) * inv_std
+    row_wait(g_src, g_all, 3)
     row_wait(x_src, x_buf, 0)
     for k in range(Z):
-        block = x_buf[k, 0:B, :].astype(F32)
-        block_gain = x_buf[k, B : B + 16, :].astype(F32)[0:8]
+        block = x_buf[k].astype(F32)
+        block_gain = g_all[k].astype(F32)[0:8]
         gains[k] = block_gain
         normed = ((block - row_mean) * inv_std) * block_gain[0:1]
         cgain[k] = normed
@@ -634,7 +673,8 @@
             VM((T, cap, B), BF), VM((T, cap, B), BF),
             VM((T, cap, B), F32), VM((T, cap, B), F32),
             VM((T, cap, B), BF), VM((T, cap, B), BF),
-            VM((B + 16, B), BF), VM((Z, B + 16, B), BF),
+            VM((16, B), BF), VM((Z, 16, B), BF),
+            VM((B, B), BF), VM((Z, B, B), BF),
             VM((B, B), BF), VM((Z, B, B), BF),
             VM((B, B), BF), VM((Z, B, B), BF),
             VM((X, B, 3 * B), BF), VM((X - 1, B, 3 * B), BF),
@@ -646,10 +686,10 @@
             VM((B, Z * B), BF), VM((Z, B, B), F32), VM((Z, 8, B), F32),
             VM((X, B, B), F32), VM((X, B, B), BF), VM((X, 16, B), BF),
             VM((3, 8, B), F32), VM((3, V, 8, B), F32),
-            dma((11,)), dma(()), dma(()), dma((X // C, 2)),
+            dma((11,)), dma((3,)), dma(()), dma((X // C, 4)),
             dma((2, X // C, 2, right)), dma((2, X // C)),
             dma((2, X // C)), dma((2, X // C)),
-            dma((4,)), dma((4,)), dma((3,)), dma((3,)),
+            dma((4,)), dma((4,)), dma((4,)), dma((4,)),
             dma((3,)), dma((3,)), dma((4,)), dma((4,)),
             dma((3,)), dma((3,)), dma((3,)), dma((3,)),
         ],

time: 134 us -> 133 us (level)
  no operation moved by 1% of the time
where the time goes in v5:
time: 133 us
  Pallas kernels  133 us (100%)
    pallas_call x1, Pallas kernels, local(): pl.pallas_call(functools.partial(main_kernel, X, Z, Y, C, vocab_rows), ou...  130 us
    pallas_call x1, Pallas kernels, local(): pl.pallas_call(functools.partial(table_kernel, tile), grid=(vocab_rows //...  3.24 us

profile of v5, /device:TPU:1, one launch (start us, length us, event | category | flops | bytes accessed | tf_op | source)
XLA Modules:
  0.0 132.9 jit_solution(3566639712056161273)
XLA Ops:
  0.0 129.7 %shard_map.109 = (bf16[256,128]{1,0:T(8,128)(2,1)}, f32[8,256]{1,0:T(8,128)}) custom-call(bf16[8192,128]{1,0:T(8,128)(2,1)} %emb_hbm.1, bf16[1,128]{1,0:T(2,128)(2,1)} %bitcast.4, bf16[256,384]{1,0:T(8,128)(2,1)} %bitcast.3, bf16[256,128]{1,0:T(8,128)(2,1)} %wo_hbm.1, bf16[256,128]{1,0:T(8,128)(2,1)} %wd_hbm.1, bf16[1,128]{1,0:T(2,128)(2,1)} %bitcast.5, ...), custom_call_target="tpu_custom_call" | custom-call | tf_op jit(solution)/shard_map/pallas_call | solution.py:655
  129.7 3.2 %shard_map.110 = bf16[8192,128]{1,0:T(8,128)(2,1)} custom-call(bf16[256,128]{1,0:T(8,128)(2,1)} %get-tuple-element.7.grad_ref, f32[8,256]{1,0:T(8,128)} %get-tuple-element.8.req_ref), custom_call_target="tpu_custom_call" | custom-call | tf_op jit(solution)/shard_map/pallas_call | solution.py:709

commit v6 on v5

--- a/solution.py
+++ b/solution.py
@@ -306,16 +306,19 @@
     row = (z + X - x) % X
     at_home = x == row
 
-    def block_done(ref, sem):
+    whole_rows, H = pl.ds(0, B), B // 2
+    halves = [(0, pl.ds(0, H)), (1, pl.ds(H, H))]
+
+    def block_done(ref, sem, rows):
         @pl.when(at_home)
         def _():
-            wait_bytes(ref.at[pl.ds(0, Z - 1)], sem)
+            wait_bytes(ref.at[pl.ds(0, Z - 1), rows], sem)
 
         @pl.when(jnp.logical_not(at_home))
         def _():
-            wait_bytes(ref, sem)
-
-    def row_start(src, buf, n):
+            wait_bytes(ref.at[pl.ds(0, Z), rows], sem)
+
+    def row_start(src, buf, n, rows=whole_rows):
         k = v // X
         for j in range(Z):
             zd = (z + far_first(j, Z)) % Z
@@ -323,43 +326,46 @@
 
             @pl.when(mine)
             def _():
-                pltpu.make_async_copy(src, buf.at[k], e_recv.at[n]).start()
+                pltpu.make_async_copy(src.at[rows], buf.at[k, rows], e_recv.at[n]).start()
 
             @pl.when(jnp.logical_not(mine))
             def _():
-                remote(src, buf.at[k], e_send.at[n], e_recv.at[n], dev(row, zd, y, c)).start()
-
-        pending.append(lambda: block_done(buf, e_send.at[n]))
-
-    def row_wait(src, buf, n):
-        wait_bytes(buf, e_recv.at[n])
-
-    def rx_start(part, buf, n):
+                to = dev(row, zd, y, c)
+                remote(src.at[rows], buf.at[k, rows], e_send.at[n], e_recv.at[n], to).start()
+
+        pending.append(lambda: block_done(buf, e_send.at[n], rows))
+
+    def row_wait(buf, n, rows=whole_rows):
+        wait_bytes(buf.at[pl.ds(0, Z), rows], e_recv.at[n])
+
+    def rx_start(part, buf, n, rows=whole_rows):
         for d in [far_first(i, X) for i in range(X - 1)]:
             to = (x + d) % X
             remote(
-                part.at[to], buf.at[d - 1], rx_send.at[n], rx_recv.at[n], dev(to, z, y, c)
+                part.at[to, rows], buf.at[d - 1, rows], rx_send.at[n], rx_recv.at[n],
+                dev(to, z, y, c),
             ).start()
-        pending.append(lambda: wait_bytes(buf, rx_send.at[n]))
-
-    def rx_sum(part, buf, n):
-        wait_bytes(buf, rx_recv.at[n])
-        total = part[x].astype(F32)
+        pending.append(lambda: wait_bytes(buf.at[pl.ds(0, X - 1), rows], rx_send.at[n]))
+
+    def rx_sum(part, buf, n, rows=whole_rows):
+        wait_bytes(buf.at[pl.ds(0, X - 1), rows], rx_recv.at[n])
+        total = part[x, rows].astype(F32)
         for d in range(1, X):
-            total = total + buf[d - 1].astype(F32)
+            total = total + buf[d - 1, rows].astype(F32)
         return total
 
-    def ax_start(buf, n):
+    def ax_start(buf, n, rows=whole_rows):
         for d in [far_first(i, X) for i in range(X - 1)]:
             remote(
-                buf.at[x], buf.at[x], ax_send.at[n], ax_recv.at[n], dev((x + d) % X, z, y, c)
+                buf.at[x, rows], buf.at[x, rows], ax_send.at[n], ax_recv.at[n],
+                dev((x + d) % X, z, y, c),
             ).start()
-        pending.append(lambda: wait_bytes(buf.at[pl.ds(0, X - 1)], ax_send.at[n]))
-
-    def ax_wait(buf, n):
-        wait_bytes(buf.at[pl.ds(0, X - 1)], ax_recv.at[n])
-
-    def own_start(part, buf, n):
+        pending.append(lambda: wait_bytes(buf.at[pl.ds(0, X - 1), rows], ax_send.at[n]))
+
+    def ax_wait(buf, n, rows=whole_rows):
+        wait_bytes(buf.at[pl.ds(0, X - 1), rows], ax_recv.at[n])
+
+    def own_start(part, buf, n, rows):
         for j in range(Z):
             zd = (z + far_first(j, Z)) % Z
             xd = (zd % X + X - x) % X
@@ -368,23 +374,25 @@
 
             @pl.when(mine)
             def _():
-                pltpu.make_async_copy(part.at[k], buf.at[z], r_recv.at[n]).start()
+                pltpu.make_async_copy(part.at[k, rows], buf.at[z, rows], r_recv.at[n]).start()
 
             @pl.when(jnp.logical_not(mine))
             def _():
                 to = dev(xd, zd, y, c)
-                remote(part.at[k], buf.at[z], r_send.at[n], r_recv.at[n], to).start()
-
-        pending.append(lambda: block_done(part, r_send.at[n]))
-
-    def own_sum(buf, n):
-        wait_bytes(buf, r_recv.at[n])
-        total = buf[0].astype(F32)
+                remote(
+                    part.at[k, rows], buf.at[z, rows], r_send.at[n], r_recv.at[n], to
+                ).start()
+
+        pending.append(lambda: block_done(part, r_send.at[n], rows))
+
+    def own_sum(buf, n, rows=whole_rows):
+        wait_bytes(buf.at[pl.ds(0, Z), rows], r_recv.at[n])
+        total = buf[0, rows].astype(F32)
         for k in range(1, Z):
-            total = total + buf[k].astype(F32)
+            total = total + buf[k, rows].astype(F32)
         return total
 
-    def spread_back(left, weights, part, buf, n, seen=None):
+    def spread_back(left, weights, part, buf, n, rows=whole_rows, seen=None):
         step = 2
         for first in range(0, Z, step):
             total = None
@@ -392,10 +400,10 @@
                 term = dot_nt(left(xx), weights(xx, pl.ds(first * B, step * B)))
                 total = term if total is None else total + term
             for k in range(first, first + step):
-                part[k] = total[:, (k - first) * B : (k - first + 1) * B].astype(BF)
+                part[k, rows] = total[:, (k - first) * B : (k - first + 1) * B].astype(BF)
         if seen is not None:
             seen()
-        own_start(part, buf, n)
+        own_start(part, buf, n, rows)
 
     def ar_start(rows, n):
         ar_src[n] = rows
@@ -416,7 +424,7 @@
     for copy in copies[6:]:
         copy.wait()
     hw_buf[x] = jnp.broadcast_to(hw_ref[...].astype(F32), (16, B)).astype(BF)
-    ax_start(hw_buf, 3)
+    ax_start(hw_buf, 3, pl.ds(0, 16))
     put_hot = jnp.where(place_hot, 1.0, 0.0).astype(BF)
     place_square = row_to_square(place)
     take_hot = jnp.concatenate(
@@ -432,7 +440,7 @@
     gain = gain_ref[...].astype(F32)
     head_vector = hw_ref[...].astype(F32)
     g_src[...] = jnp.broadcast_to(gain, (16, B)).astype(BF)
-    row_start(g_src, g_all, 3)
+    row_start(g_src, g_all, 3, pl.ds(0, 16))
     tok_wait(ids_src, ids_buf, 0)
     requested = ids_buf[...].reshape(R, B)
     chunk = 512
@@ -490,8 +498,8 @@
     variance = stats[:, 1:2] / D - row_mean * row_mean
     inv_std = lax.rsqrt(variance + epsilon)
     centered = (features - row_mean) * inv_std
-    row_wait(g_src, g_all, 3)
-    row_wait(x_src, x_buf, 0)
+    row_wait(g_all, 3, pl.ds(0, 16))
+    row_wait(x_buf, 0)
     for k in range(Z):
         block = x_buf[k].astype(F32)
         block_gain = g_all[k].astype(F32)[0:8]
@@ -517,27 +525,33 @@
     probabilities = exps / jnp.sum(exps, axis=-1, keepdims=True)
     prob_rounded = probabilities.astype(BF)
     h_src[...] = dot(prob_rounded, values).astype(BF)
-    row_start(h_src, h_buf, 1)
+    for n, rows in halves:
+        row_start(h_src, h_buf, 1 + 3 * n, rows)
     for h in (3, 4):
         w2_forward(1, 0, h)
         w2_forward(1, 1, h)
-    row_wait(h_src, h_buf, 1)
     w2_ready(1)
 
-    heads_row = jnp.concatenate([h_buf[k] for k in range(Z)], axis=1)
-    for xx in range(X):
-        po[xx] = dot(heads_row, Wod[xx, :, 0:B]).astype(po.dtype)
-    rx_start(po, po_buf, 1)
-    hidden = features + rx_sum(po, po_buf, 1)
-    d_src[...] = hidden.astype(BF)
-    row_start(d_src, d_buf, 2)
-    row_wait(d_src, d_buf, 2)
-
-    dense_row = jnp.concatenate([d_buf[k] for k in range(Z)], axis=1)
-    for xx in range(X):
-        pd[xx] = dot(dense_row, Wod[xx, :, B : 2 * B]).astype(pd.dtype)
-    rx_start(pd, pd_buf, 2)
-    dense_linear = rx_sum(pd, pd_buf, 2)
+    for n, rows in halves:
+        row_wait(h_buf, 1 + 3 * n, rows)
+        heads_row = jnp.concatenate([h_buf[k, rows] for k in range(Z)], axis=1)
+        for xx in range(X):
+            po[xx, rows] = dot(heads_row, Wod[xx, :, 0:B]).astype(po.dtype)
+        rx_start(po, po_buf, 1 + 2 * n, rows)
+    for n, rows in halves:
+        hidden = features[n * H : (n + 1) * H] + rx_sum(po, po_buf, 1 + 2 * n, rows)
+        d_src[rows] = hidden.astype(BF)
+        row_start(d_src, d_buf, 2 + 3 * n, rows)
+
+    for n, rows in halves:
+        row_wait(d_buf, 2 + 3 * n, rows)
+        dense_row = jnp.concatenate([d_buf[k, rows] for k in range(Z)], axis=1)
+        for xx in range(X):
+            pd[xx, rows] = dot(dense_row, Wod[xx, :, B : 2 * B]).astype(pd.dtype)
+        rx_start(pd, pd_buf, 2 + 2 * n, rows)
+    dense_linear = jnp.concatenate(
+        [rx_sum(pd, pd_buf, 2 + 2 * n, rows) for n, rows in halves], axis=0
+    )
     dl_buf[x] = dense_linear
     activated = dense_linear * (0.5 * (1.0 + lax.erf(dense_linear * inv_root_two)))
     ar_start(
@@ -552,7 +566,7 @@
         1,
     )
     ax_start(dl_buf, 0)
-    ax_wait(hw_buf, 3)
+    ax_wait(hw_buf, 3, pl.ds(0, 16))
     ax_wait(dl_buf, 0)
     gelus = []
     for xx in range(X):
@@ -574,13 +588,28 @@
             logit_grads * vector - mean_grads - head_centered * mean_product
         )
         pre[xx] = (activated_grads * slope).astype(BF)
-    spread_back(lambda xx: pre[xx], lambda xx, rows: Wod[xx, rows, B : 2 * B], b1, b1_buf, 0)
-    hidden_grads = own_sum(b1_buf, 0)
-    hr_buf[x] = hidden_grads.astype(BF)
-    ax_start(hr_buf, 1)
-    ax_wait(hr_buf, 1)
-    spread_back(lambda xx: hr_buf[xx], lambda xx, rows: Wod[xx, rows, 0:B], b2, b2_buf, 1)
-    out_rounded = own_sum(b2_buf, 1).astype(BF)
+    for n, rows in halves:
+        spread_back(
+            lambda xx: pre[xx, rows],
+            lambda xx, part: Wod[xx, part, B : 2 * B],
+            b1, b1_buf, 3 * n, rows,
+        )
+    pieces = []
+    for n, rows in halves:
+        pieces.append(own_sum(b1_buf, 3 * n, rows))
+        hr_buf[x, rows] = pieces[n].astype(BF)
+        ax_start(hr_buf, 1 + 3 * n, rows)
+    for n, rows in halves:
+        ax_wait(hr_buf, 1 + 3 * n, rows)
+        spread_back(
+            lambda xx: hr_buf[xx, rows],
+            lambda xx, part: Wod[xx, part, 0:B],
+            b2, b2_buf, 1 + 3 * n, rows,
+        )
+    hidden_grads = jnp.concatenate(pieces, axis=0)
+    out_rounded = jnp.concatenate(
+        [own_sum(b2_buf, 1 + 3 * n, rows) for n, rows in halves], axis=0
+    ).astype(BF)
 
     prob_grads = dot_nt(out_rounded, values)
     value_grads = dot_tn(prob_rounded, out_rounded)
@@ -610,7 +639,7 @@
         for done in old:
             done()
 
-    spread_back(lambda xx: g_buf[xx], lambda xx, rows: Wq[xx, rows, :], b3, b3_buf, 2, send_sums)
+    spread_back(lambda xx: g_buf[xx], lambda xx, rows: Wq[xx, rows, :], b3, b3_buf, 2, seen=send_sums)
     finish_old()
     scaled = own_sum(b3_buf, 2) * gain
     stats = ar_sum(2)
@@ -689,9 +718,9 @@
             dma((11,)), dma((3,)), dma(()), dma((X // C, 4)),
             dma((2, X // C, 2, right)), dma((2, X // C)),
             dma((2, X // C)), dma((2, X // C)),
-            dma((4,)), dma((4,)), dma((4,)), dma((4,)),
-            dma((3,)), dma((3,)), dma((4,)), dma((4,)),
-            dma((3,)), dma((3,)), dma((3,)), dma((3,)),
+            dma((4,)), dma((4,)), dma((6,)), dma((6,)),
+            dma((5,)), dma((5,)), dma((5,)), dma((5,)),
+            dma((5,)), dma((5,)), dma((3,)), dma((3,)),
         ],
         compiler_params=pltpu.CompilerParams(
             collective_id=0, has_side_effects=True, vmem_limit_bytes=60 * 1024 * 1024

time: 133 us -> 132 us (level)
    pallas_call x1, Pallas kernels: 130 us -> 128 us  [local(): pl.pallas_call(functools.partial(main_kernel, X, Z, Y, C, vocab_rows), ou...]
where the time goes in v6:
time: 132 us
  Pallas kernels  132 us (100%)
    pallas_call x1, Pallas kernels, local(): pl.pallas_call(functools.partial(main_kernel, X, Z, Y, C, vocab_rows), ou...  128 us
    pallas_call x1, Pallas kernels, local(): pl.pallas_call(functools.partial(table_kernel, tile), grid=(vocab_rows //...  3.24 us

profile of v6, /device:TPU:1, one launch (start us, length us, event | category | flops | bytes accessed | tf_op | source)
XLA Modules:
  0.0 131.5 jit_solution(6352763325889838887)
XLA Ops:
  0.0 128.3 %shard_map.109 = (bf16[256,128]{1,0:T(8,128)(2,1)}, f32[8,256]{1,0:T(8,128)}) custom-call(bf16[8192,128]{1,0:T(8,128)(2,1)} %emb_hbm.1, bf16[1,128]{1,0:T(2,128)(2,1)} %bitcast.4, bf16[256,384]{1,0:T(8,128)(2,1)} %bitcast.3, bf16[256,128]{1,0:T(8,128)(2,1)} %wo_hbm.1, bf16[256,128]{1,0:T(8,128)(2,1)} %wd_hbm.1, bf16[1,128]{1,0:T(2,128)(2,1)} %bitcast.5, ...), custom_call_target="tpu_custom_call" | custom-call | tf_op jit(solution)/shard_map/pallas_call | solution.py:684
  128.3 3.2 %shard_map.110 = bf16[8192,128]{1,0:T(8,128)(2,1)} custom-call(bf16[256,128]{1,0:T(8,128)(2,1)} %get-tuple-element.7.grad_ref, f32[8,256]{1,0:T(8,128)} %get-tuple-element.8.req_ref), custom_call_target="tpu_custom_call" | custom-call | tf_op jit(solution)/shard_map/pallas_call | solution.py:738

commit v7 on v6

--- a/solution.py
+++ b/solution.py
@@ -338,13 +338,15 @@
     def row_wait(buf, n, rows=whole_rows):
         wait_bytes(buf.at[pl.ds(0, Z), rows], e_recv.at[n])
 
-    def rx_start(part, buf, n, rows=whole_rows):
-        for d in [far_first(i, X) for i in range(X - 1)]:
+    def rx_start(left, weights, part, buf, n, rows=whole_rows):
+        for d in [far_first(i, X) for i in range(X)]:
             to = (x + d) % X
-            remote(
-                part.at[to, rows], buf.at[d - 1, rows], rx_send.at[n], rx_recv.at[n],
-                dev(to, z, y, c),
-            ).start()
+            part[to, rows] = dot(left, weights(to)).astype(BF)
+            if d:
+                remote(
+                    part.at[to, rows], buf.at[d - 1, rows], rx_send.at[n], rx_recv.at[n],
+                    dev(to, z, y, c),
+                ).start()
         pending.append(lambda: wait_bytes(buf.at[pl.ds(0, X - 1), rows], rx_send.at[n]))
 
     def rx_sum(part, buf, n, rows=whole_rows):
@@ -512,9 +514,7 @@
     w2_forward(1, 0, 1)
     w2_forward(1, 1, 1)
     w2_ready(0)
-    for xx in range(X):
-        pq[xx] = dot(nrm[...], Wq[xx]).astype(BF)
-    rx_start(pq, pq_buf, 0)
+    rx_start(nrm[...], lambda to: Wq[to], pq, pq_buf, 0)
     w2_forward(1, 0, 2)
     w2_forward(1, 1, 2)
     qkv = rx_sum(pq, pq_buf, 0).astype(BF)
@@ -535,9 +535,7 @@
     for n, rows in halves:
         row_wait(h_buf, 1 + 3 * n, rows)
         heads_row = jnp.concatenate([h_buf[k, rows] for k in range(Z)], axis=1)
-        for xx in range(X):
-            po[xx, rows] = dot(heads_row, Wod[xx, :, 0:B]).astype(po.dtype)
-        rx_start(po, po_buf, 1 + 2 * n, rows)
+        rx_start(heads_row, lambda to: Wod[to, :, 0:B], po, po_buf, 1 + 2 * n, rows)
     for n, rows in halves:
         hidden = features[n * H : (n + 1) * H] + rx_sum(po, po_buf, 1 + 2 * n, rows)
         d_src[rows] = hidden.astype(BF)
@@ -546,9 +544,7 @@
     for n, rows in halves:
         row_wait(d_buf, 2 + 3 * n, rows)
         dense_row = jnp.concatenate([d_buf[k, rows] for k in range(Z)], axis=1)
-        for xx in range(X):
-            pd[xx, rows] = dot(dense_row, Wod[xx, :, B : 2 * B]).astype(pd.dtype)
-        rx_start(pd, pd_buf, 2 + 2 * n, rows)
+        rx_start(dense_row, lambda to: Wod[to, :, B : 2 * B], pd, pd_buf, 2 + 2 * n, rows)
     dense_linear = jnp.concatenate(
         [rx_sum(pd, pd_buf, 2 + 2 * n, rows) for n, rows in halves], axis=0
     )

time: 132 us -> 130 us (0.985)
  Pallas kernels: 132 us -> 130 us
    pallas_call x1, Pallas kernels: 128 us -> 127 us  [local(): pl.pallas_call(functools.partial(main_kernel, X, Z, Y, C, vocab_rows), ou...]
where the time goes in v7:
time: 130 us
  Pallas kernels  130 us (100%)
    pallas_call x1, Pallas kernels, local(): pl.pallas_call(functools.partial(main_kernel, X, Z, Y, C, vocab_rows), ou...  127 us
    pallas_call x1, Pallas kernels, local(): pl.pallas_call(functools.partial(table_kernel, tile), grid=(vocab_rows //...  3.24 us

profile of v7, /device:TPU:1, one launch (start us, length us, event | category | flops | bytes accessed | tf_op | source)
XLA Modules:
  0.0 129.9 jit_solution(3073112023136323273)
XLA Ops:
  0.0 126.7 %shard_map.109 = (bf16[256,128]{1,0:T(8,128)(2,1)}, f32[8,256]{1,0:T(8,128)}) custom-call(bf16[8192,128]{1,0:T(8,128)(2,1)} %emb_hbm.1, bf16[1,128]{1,0:T(2,128)(2,1)} %bitcast.4, bf16[256,384]{1,0:T(8,128)(2,1)} %bitcast.3, bf16[256,128]{1,0:T(8,128)(2,1)} %wo_hbm.1, bf16[256,128]{1,0:T(8,128)(2,1)} %wd_hbm.1, bf16[1,128]{1,0:T(2,128)(2,1)} %bitcast.5, ...), custom_call_target="tpu_custom_call" | custom-call | tf_op jit(solution)/shard_map/pallas_call | solution.py:680
  126.7 3.2 %shard_map.110 = bf16[8192,128]{1,0:T(8,128)(2,1)} custom-call(bf16[256,128]{1,0:T(8,128)(2,1)} %get-tuple-element.7.grad_ref, f32[8,256]{1,0:T(8,128)} %get-tuple-element.8.req_ref), custom_call_target="tpu_custom_call" | custom-call | tf_op jit(solution)/shard_map/pallas_call | solution.py:734
